TPU v7x, 256 devices: a whole 4x4x8 slice. The times are simulated.
256 devices in a mesh: dp: 2 (over x_hi), fsdp: 16 (over x_lo, y, core), tensor: 8 (over z).
Axes of the slice: x: 4 (x_hi: 2, x_lo: 2; x = x_hi * 2 + x_lo), y: 4, z: 8, core: 2. Of those that a mesh axis runs over, the one named last changes fastest.
Arguments:
- residual_input: bfloat16 [2, 512, 16384], P('dp', 'tensor', 'fsdp'), may hold values from -6 to 6
- block_output_gradient: bfloat16 [2, 512, 16384], P('dp', 'tensor', 'fsdp'), may hold values from -6 to 6
- norm_gain_vector: float32 [16384], P('fsdp'), may hold values from 0.5 to 1.5
- query_matrix: bfloat16 [16384, 8, 2048], P('fsdp', 'tensor'), may hold values from -0.046875 to 0.046875
- keyvalue_matrix: bfloat16 [16384, 2, 1024], P('fsdp', None, 'tensor'), may hold values from -0.046875 to 0.046875
- output_matrix: bfloat16 [8, 2048, 16384], P('tensor', None, 'fsdp'), may hold values from -0.046875 to 0.046875
- adapter_projection_down: bfloat16 [16384, 192], P('fsdp'), may hold values from -0.046875 to 0.046875
- adapter_query_up: bfloat16 [64, 8, 2048], P(None, 'tensor', 'fsdp'), may hold values from -0.75 to 0.75
- adapter_keyvalue_up: bfloat16 [64, 2, 1024], P(None, None, 'tensor'), may hold values from -0.75 to 0.75
- adapter_output_down: bfloat16 [8, 2048, 64], P('tensor', 'fsdp'), may hold values from -0.046875 to 0.046875
- adapter_output_up: bfloat16 [64, 16384], P(None, 'fsdp'), may hold values from -0.75 to 0.75
Outputs:
- grad_hidden: float32 [2, 512, 16384], P('dp', 'tensor', 'fsdp')
- projection_down_gradient: float32 [16384, 192], P('fsdp')
- query_up_gradient: float32 [64, 8, 2048], P(None, 'tensor', 'fsdp')
- keyvalue_up_gradient: float32 [64, 2, 1024], P(None, None, 'tensor')
- output_down_gradient: float32 [8, 2048, 64], P('tensor', 'fsdp')
- output_up_gradient: float32 [64, 16384], P(None, 'fsdp')
All inputs are finite; a program needn't handle non-finite values.
Results may differ from a plain program's by a relative error of at most 0.025.
The roundings to bfloat16 on the way count: a program that leaves them out, or rounds other values in their place, can miss the bound.
Values may be sent and summed in bfloat16 or wider, within the bound.
A program may use at most 64 MiB of HBM per device.

v0:
```python
import math

import jax
import jax.numpy as jnp
from jax import lax
from jax.sharding import PartitionSpec as P

eps = 1e-05
adapter_scale = 2.0
theta = 500000.0


def rope_tables(length, width_total):
    half = width_total // 2
    freq = theta ** (-(jnp.arange(half, dtype=jnp.float32) * 2.0) / width_total)
    angles = jnp.arange(length, dtype=jnp.float32)[:, None] * freq[None, :]
    return (jnp.cos(angles), jnp.sin(angles))


def rotate(value_rows, cosine, sine):
    half = value_rows.shape[-1] // 2
    first = value_rows[..., :half]
    second = value_rows[..., half:]
    return jnp.concatenate(
        [first * cosine - second * sine, second * cosine + first * sine], axis=-1
    )


def rotate_back(grads, cosine, sine):
    half = grads.shape[-1] // 2
    first = grads[..., :half]
    second = grads[..., half:]
    return jnp.concatenate(
        [first * cosine + second * sine, second * cosine - first * sine], axis=-1
    )


def contract_product(left, right, left_dim, right_dim):
    return lax.dot_general(
        left, right, (((left_dim,), (right_dim,)), ((), ())), preferred_element_type=jnp.float32
    )


def local(
    residual_input,
    block_output_gradient,
    norm_gain_vector,
    query_matrix,
    keyvalue_matrix,
    output_matrix,
    adapter_projection_down,
    adapter_query_up,
    adapter_keyvalue_up,
    adapter_output_down,
    adapter_output_up,
):
    single_float_type = jnp.float32
    brain_float_type = jnp.bfloat16
    tensor_pos = lax.axis_index("tensor")
    fsdp_pos = lax.axis_index("fsdp")
    hidden_shard = residual_input[0].astype(single_float_type)
    rows_own = hidden_shard.shape[0]
    model_width_total = hidden_shard.shape[1] * lax.axis_size("fsdp")
    adapter_rank = adapter_projection_down.shape[1] // 3
    width_total = keyvalue_matrix.shape[2]
    squares = lax.psum(jnp.sum(hidden_shard * hidden_shard, axis=-1), "fsdp")
    inverse_deviation = lax.rsqrt(squares / model_width_total + eps)[:, None]
    hidden_normalized = hidden_shard * inverse_deviation
    normed_shard = (hidden_normalized * norm_gain_vector).astype(brain_float_type)
    normed_hidden = lax.all_gather(normed_shard, "tensor", axis=0, tiled=True)
    output_gradient_shard = block_output_gradient[0]
    output_gradient = lax.all_gather(output_gradient_shard, "tensor", axis=0, tiled=True)
    length = normed_hidden.shape[0]
    qweight = query_matrix[:, 0, :]
    oweight = output_matrix[0]
    block = qweight
    query_columns = lax.psum_scatter(
        contract_product(block, normed_hidden, 0, 1), "fsdp", scatter_dimension=0, tiled=True
    )
    kvweight = keyvalue_matrix.reshape(keyvalue_matrix.shape[0], 2 * width_total)
    kv_part = jnp.dot(normed_hidden, kvweight, preferred_element_type=single_float_type)
    lowrank_piece = jnp.dot(
        normed_hidden, adapter_projection_down, preferred_element_type=single_float_type
    )
    keyvalue_total, low_sum = lax.psum((kv_part, lowrank_piece), "fsdp")
    lowrank_input = low_sum.astype(brain_float_type)
    lowrank_query = lowrank_input[:, :adapter_rank]
    lowrank_key = lowrank_input[:, adapter_rank : 2 * adapter_rank]
    lowrank_value = lowrank_input[:, 2 * adapter_rank :]
    query_up_matrix = adapter_query_up[:, 0, :]
    key_up_matrix = adapter_keyvalue_up[:, 0, :]
    value_up_matrix = adapter_keyvalue_up[:, 1, :]
    query_rows = query_columns.T + adapter_scale * jnp.dot(
        lowrank_query, query_up_matrix, preferred_element_type=single_float_type
    )
    key_rows = keyvalue_total[:, :width_total] + adapter_scale * jnp.dot(
        lowrank_key, key_up_matrix, preferred_element_type=single_float_type
    )
    value_rows = keyvalue_total[:, width_total:] + adapter_scale * jnp.dot(
        lowrank_value, value_up_matrix, preferred_element_type=single_float_type
    )
    cosine, sine = rope_tables(length, width_total)
    qrot = rotate(query_rows, cosine, sine).astype(brain_float_type)
    krot = rotate(key_rows, cosine, sine).astype(brain_float_type)
    vals = value_rows.astype(brain_float_type)
    scale = 1.0 / math.sqrt(width_total)
    causal = jnp.arange(length)[:, None] >= jnp.arange(length)[None, :]
    scores = contract_product(qrot, krot, 1, 1) * scale
    scores = jnp.where(causal, scores, -1e30)
    probs = jax.nn.softmax(scores, axis=-1)
    probs_b = probs.astype(brain_float_type)
    attention_output = jnp.dot(probs_b, vals, preferred_element_type=single_float_type).astype(
        brain_float_type
    )
    output_down_matrix = adapter_output_down[0]
    low_term = jnp.dot(
        attention_output, output_down_matrix, preferred_element_type=single_float_type
    )
    backward_piece = contract_product(output_gradient, adapter_output_up, 1, 1)
    lowrank_output = lax.psum(low_term, ("fsdp", "tensor"))
    backward_output = lax.psum(backward_piece, "fsdp")
    lowrank_output = lowrank_output.astype(brain_float_type)
    backward_output = backward_output.astype(brain_float_type)
    output_up_gradient = adapter_scale * contract_product(lowrank_output, output_gradient, 0, 0)
    output_down_gradient = adapter_scale * contract_product(attention_output, backward_output, 0, 0)
    block = oweight
    attention_gradient_columns = lax.psum_scatter(
        contract_product(block, output_gradient, 1, 1), "fsdp", scatter_dimension=0, tiled=True
    )
    attention_gradient = (
        attention_gradient_columns.T
        + adapter_scale * contract_product(backward_output, output_down_matrix, 1, 1)
    ).astype(brain_float_type)
    dprobs = contract_product(attention_gradient, vals, 1, 1)
    dval = contract_product(probs_b, attention_gradient, 0, 0)
    delta = jnp.sum(probs * dprobs, axis=-1, keepdims=True)
    dscore = (probs * (dprobs - delta) * scale).astype(brain_float_type)
    dquery = jnp.dot(dscore, krot, preferred_element_type=single_float_type)
    dkey = contract_product(dscore, qrot, 0, 0)
    kv_grads = lax.psum(jnp.stack([dkey, dval], axis=1), "fsdp")
    query_gradient = rotate_back(dquery, cosine, sine).astype(brain_float_type)
    key_gradient = rotate_back(kv_grads[:, 0, :], cosine, sine).astype(brain_float_type)
    value_gradient = kv_grads[:, 1, :].astype(brain_float_type)
    keep_lead = (fsdp_pos == 0).astype(single_float_type)
    back_q = contract_product(query_gradient, query_up_matrix, 1, 1)
    back_k = contract_product(key_gradient, key_up_matrix, 1, 1) * keep_lead
    back_v = contract_product(value_gradient, value_up_matrix, 1, 1) * keep_lead
    backward_input = lax.psum(
        jnp.concatenate([back_q, back_k, back_v], axis=1), ("fsdp", "tensor")
    ).astype(brain_float_type)
    projection_down_gradient = adapter_scale * contract_product(normed_hidden, backward_input, 0, 0)
    query_up_gradient = adapter_scale * contract_product(lowrank_query, query_gradient, 0, 0)
    keyvalue_up_gradient = adapter_scale * jnp.stack(
        [
            contract_product(lowrank_key, key_gradient, 0, 0),
            contract_product(lowrank_value, value_gradient, 0, 0),
        ],
        axis=1,
    )
    dq_group = lax.all_gather(query_gradient, "fsdp", axis=1, tiled=True)
    dkv_flat = jnp.concatenate([key_gradient, value_gradient], axis=1)
    normed_gradient = lax.psum_scatter(
        contract_product(dq_group, qweight, 1, 1) + contract_product(dkv_flat, kvweight, 1, 1),
        "tensor",
        scatter_dimension=0,
        tiled=True,
    )
    shard_backward = lax.dynamic_slice_in_dim(backward_input, tensor_pos * rows_own, rows_own, 0)
    normed_gradient = normed_gradient + adapter_scale * contract_product(
        shard_backward, adapter_projection_down, 1, 1
    )
    normalized_gradient = normed_gradient * norm_gain_vector
    inner_product = lax.psum(jnp.sum(normalized_gradient * hidden_normalized, axis=-1), "fsdp")
    hidden_gradient = output_gradient_shard.astype(single_float_type) + inverse_deviation * (
        normalized_gradient - hidden_normalized * (inner_product / model_width_total)[:, None]
    )
    (
        projection_down_gradient,
        query_up_gradient,
        keyvalue_up_gradient,
        output_down_gradient,
        output_up_gradient,
    ) = lax.psum(
        (
            projection_down_gradient,
            query_up_gradient,
            keyvalue_up_gradient,
            output_down_gradient,
            output_up_gradient,
        ),
        "dp",
    )
    return (
        hidden_gradient[None],
        projection_down_gradient,
        query_up_gradient[:, None, :],
        keyvalue_up_gradient,
        output_down_gradient[None],
        output_up_gradient,
    )


def solution(mesh):
    in_specs = (
        P("dp", "tensor", "fsdp"),
        P("dp", "tensor", "fsdp"),
        P("fsdp"),
        P("fsdp", "tensor", None),
        P("fsdp", None, "tensor"),
        P("tensor", None, "fsdp"),
        P("fsdp", None),
        P(None, "tensor", "fsdp"),
        P(None, None, "tensor"),
        P("tensor", "fsdp", None),
        P(None, "fsdp"),
    )
    out_specs = (
        P("dp", "tensor", "fsdp"),
        P("fsdp", None),
        P(None, "tensor", "fsdp"),
        P(None, None, "tensor"),
        P("tensor", "fsdp", None),
        P(None, "fsdp"),
    )
    return jax.shard_map(local, mesh=mesh, in_specs=in_specs, out_specs=out_specs, check_vma=False)
```

profile of v0, /device:TPU:1, one launch (start us, length us, event | category | flops | bytes accessed | tf_op | source)
XLA Modules:
  0.0 1234.4 jit_solution(3020137691407159265)
XLA Ops:
  8.3 29.7 %psum.91 = f32[64]{0:T(128)S(1)} all-reduce(f32[64]{0:T(128)S(1)} %fusion.40), channel_id=1, replica_groups=mesh['dp'=2,'fsdp'=16,'tensor'=8] {'fsdp'}, use_global_device_ids=true, to_apply=%region_1.0 | all-reduce | flops 64 | bytes 512 | tf_op jit(solution)/shard_map/psum | solution.py:66
  41.0 34.6 %all-gather.5.cloned.1.call-done = bf16[512,1024]{1,0:T(8,128)(2,1)} async-done(((bf16[64,1024]{1,0:T(8,128)(2,1)}), bf16[512,1024]{1,0:T(8,128)(2,1)}) %all-gather.5.cloned.1.call-update) | async-done | bytes 1048592 | tf_op jit(solution)/shard_map/all_gather | solution.py:70
  75.7 2.6 fusion.26
  78.3 6.8 fusion.6
  85.2 29.4 %all-gather.9.cloned.1.call-done = bf16[1,512,1024]{2,1,0:T(8,128)(2,1)} async-done(((bf16[1,64,1024]{2,1,0:T(8,128)(2,1)}), bf16[1,512,1024]{2,1,0:T(8,128)(2,1)}) %all-gather.9.cloned.1.call-update) | async-done | bytes 1048592 | tf_op jit(solution)/shard_map/all_gather | solution.py:72
  114.7 6.8 fusion
  123.7 59.7 %all-reduce.18 = (bf16[512,64]{0,1:T(8,128)(2,1)}, bf16[512,192]{0,1:T(8,128)(2,1)S(1)}) all-reduce(f32[512,64]{0,1:T(8,128)S(1)} %fusion.20, f32[512,192]{0,1:T(8,128)S(1)} %fusion.80), channel_id=1, replica_groups=mesh['dp'=2,'fsdp'=16,'tensor'=8] {'fsdp'}, use_global_device_ids=true, to_apply=%region_8.9 | all-reduce | flops 131072 | bytes 786432 | tf_op jit(solution)/shard_map/psum | solution.py:121
  183.5 60.7 %all-reduce.11.cloned.1.call-done = f32[512,256]{1,0:T(8,128)} async-done(((f32[512,256]{1,0:T(8,128)}), f32[512,256]{1,0:T(8,128)}) %all-reduce.11.cloned.1.call-update) | async-done | bytes 524304 | tf_op jit(solution)/shard_map/psum | solution.py:85
  246.5 67.4 %reduce-scatter.4.cloned.1.call-done = f32[128,512]{0,1:T(8,128)} async-done(((f32[2048,512]{0,1:T(8,128)}), f32[128,512]{0,1:T(8,128)}) %reduce-scatter.4.cloned.1.call-update) | async-done | bytes 262160 | tf_op jit(solution)/shard_map/reduce_scatter | solution.py:77
  315.0 1.8 subtract_convert_fusion.3
  317.7 66.8 %reduce-scatter.6.cloned.1.call-done = f32[128,512]{0,1:T(8,128)} async-done(((f32[2048,512]{0,1:T(8,128)}), f32[128,512]{0,1:T(8,128)}) %reduce-scatter.6.cloned.1.call-update) | async-done | bytes 262160 | tf_op jit(solution)/shard_map/reduce_scatter | solution.py:127
  389.5 124.4 %all-reduce.13.cloned.1.call-done = f32[512,2,128]{2,0,1:T(8,128)} async-done(((f32[512,2,128]{2,0,1:T(8,128)}), f32[512,2,128]{2,0,1:T(8,128)}) %all-reduce.13.cloned.1.call-update) | async-done | bytes 524304 | tf_op jit(solution)/shard_map/psum | solution.py:140
  514.8 1.8 add_convert_fusion
  517.5 2.6 online-softmax
  526.5 549.4 %all-reduce.19 = (bf16[512,192]{0,1:T(8,128)(2,1)}, bf16[512,64]{1,0:T(8,128)(2,1)}) all-reduce(f32[512,192]{0,1:T(8,128)S(1)} %pad_maximum_fusion.1, f32[512,64]{1,0:T(8,128)S(1)} %fusion.52), channel_id=1, replica_groups=mesh['dp'=2,'fsdp'=16,'tensor'=8] {'fsdp','tensor'}, use_global_device_ids=true, to_apply=%region_12.13 | all-reduce | flops 131072 | bytes 786432 | tf_op jit(solution)/shard_map/psum | solution.py:148
  1075.9 1.9 convolution_multiply_fusion.7
  1077.8 2.2 convolution_multiply_fusion.1
  1080.1 5.2 fusion.2
  1085.5 1.8 convolution_add_fusion
  1089.8 51.2 %all-reduce.17.cloned.1.call-done = (f32[1024,192]{0,1:T(8,128)}, f32[64,2,128]{2,0,1:T(8,128)}, f32[64,1024]{1,0:T(8,128)}) async-done(((f32[1024,192]{0,1:T(8,128)}, f32[64,2,128]{2,0,1:T(8,128)}, f32[64,1024]{1,0:T(8,128)}), (f32[1024,192]{0,1:T(8,128)}, f32[64,2,128]{2,0,1:T(8,128)}, f32[64,1024]{1,0:T(8,128)})) %all-reduce.17.cloned.1.call-update) | async-done | bytes 1114128 | tf_op jit(solution)/shard_map/psum | solution.py:183
  1142.5 38.8 %reduce-scatter.8.cloned.1.call-done = f32[64,1024]{1,0:T(8,128)} async-done(((f32[512,1024]{1,0:T(8,128)}), f32[64,1024]{1,0:T(8,128)}) %reduce-scatter.8.cloned.1.call-update) | async-done | bytes 262160 | tf_op jit(solution)/shard_map/reduce_scatter | solution.py:162
  1182.7 31.2 %psum.97 = f32[64]{0:T(128)S(1)} all-reduce(f32[64]{0:T(128)S(1)} %get-tuple-element.45), channel_id=1, replica_groups=mesh['dp'=2,'fsdp'=16,'tensor'=8] {'fsdp'}, use_global_device_ids=true, to_apply=%region_14.15 | all-reduce | flops 64 | bytes 512 | tf_op jit(solution)/shard_map/psum | solution.py:173
  1214.8 6.2 all-reduce.15.cloned.1.call-done
  1221.0 2.1 copy.77
  (112 shorter events, 34.4 us)
Async XLA Ops:
  7.2 115.1 %copy-start = (bf16[1024,192]{0,1:T(8,128)(2,1)S(1)}, bf16[1024,192]{0,1:T(8,128)(2,1)}, u32[]{:S(2)}) copy-start(bf16[1024,192]{0,1:T(8,128)(2,1)} %param.17) | copy-start | bytes 1179652
  7.2 68.5 %all-gather.5.cloned.1.call-start = ((), (), s32[]{:S(2)}) async-start(), calls=%async_computation.3 | async-start | bytes 1179648 | tf_op jit(solution)/shard_map/all_gather | solution.py:70
  40.2 74.5 %all-gather.9.cloned.1.call-start = ((), (), s32[]{:S(2)}) async-start(), calls=%async_computation.10 | async-start | bytes 1179648 | tf_op jit(solution)/shard_map/all_gather | solution.py:72
  41.0 203.2 %all-reduce.11.cloned.1.call-start = ((), (), s32[]{:S(2)}) async-start(), calls=%async_computation.5 | async-start | bytes 1048576 | tf_op jit(solution)/shard_map/psum | solution.py:85
  78.3 235.6 %reduce-scatter.4.cloned.1.call-start = ((), (), s32[]{:S(2)}) async-start(), calls=%async_computation.4 | async-start | bytes 4456448 | tf_op jit(solution)/shard_map/reduce_scatter | solution.py:77
  85.2 299.3 %reduce-scatter.6.cloned.1.call-start = ((), (), s32[]{:S(2)}) async-start(), calls=%async_computation.6 | async-start | bytes 4456448 | tf_op jit(solution)/shard_map/reduce_scatter | solution.py:127
  121.5 192.4 %copy-start.19 = (bf16[64,1,128]{2,0,1:T(8,128)(2,1)S(1)}, bf16[64,1,128]{2,0,1:T(8,128)(2,1)}, u32[]{:S(2)}) copy-start(bf16[64,1,128]{2,0,1:T(8,128)(2,1)} %param.18) | copy-start | bytes 49156
  121.5 392.3 %all-reduce.13.cloned.1.call-start = ((), (), s32[]{:S(2)}) async-start(), calls=%async_computation.8 | async-start | bytes 1048576 | tf_op jit(solution)/shard_map/psum | solution.py:140
  122.7 191.1 %copy-start.15 = (bf16[64,1,128]{2,1,0:T(2,128)(2,1)}, bf16[64,1,128]{2,1,0:T(2,128)(2,1)S(1)}, u32[]{:S(2)}) copy-start(bf16[64,1,128]{2,1,0:T(2,128)(2,1)S(1)} %get-tuple-element.36) | copy-start | bytes 49156
  122.7 191.1 %copy-start.17 = (bf16[64,1,128]{2,1,0:T(2,128)(2,1)}, bf16[64,1,128]{2,1,0:T(2,128)(2,1)S(1)}, u32[]{:S(2)}) copy-start(bf16[64,1,128]{2,1,0:T(2,128)(2,1)S(1)} %get-tuple-element.35) | copy-start | bytes 49156
  183.5 133.4 %copy-start.9 = (bf16[512,192]{0,1:T(8,128)(2,1)}, bf16[512,192]{0,1:T(8,128)(2,1)S(1)}, u32[]{:S(2)}) copy-start(bf16[512,192]{0,1:T(8,128)(2,1)S(1)} %get-tuple-element.21) | copy-start | bytes 589828
  246.5 139.7 %copy-start.8 = (f32[512,128]{1,0:T(8,128)}, f32[512,128]{1,0:T(8,128)S(1)}, u32[]{:S(2)}) copy-start(f32[512,128]{1,0:T(8,128)S(1)} %fusion.12) | copy-start | bytes 786436
  388.1 132.0 %copy-start.20 = (bf16[1,128,64]{1,2,0:T(8,128)(2,1)S(1)}, bf16[1,128,64]{1,2,0:T(8,128)(2,1)}, u32[]{:S(2)}) copy-start(bf16[1,128,64]{1,2,0:T(8,128)(2,1)} %param.20) | copy-start | bytes 49156
  388.1 133.1 %copy-start.18 = (bf16[64,1,128]{2,1,0:T(2,128)(2,1)S(1)}, bf16[64,1,128]{2,1,0:T(2,128)(2,1)}, u32[]{:S(2)}) copy-start(bf16[64,1,128]{2,1,0:T(2,128)(2,1)} %copy-done.17) | copy-start | bytes 49156
  388.2 135.4 %copy-start.16 = (bf16[64,1,128]{2,1,0:T(2,128)(2,1)S(1)}, bf16[64,1,128]{2,1,0:T(2,128)(2,1)}, u32[]{:S(2)}) copy-start(bf16[64,1,128]{2,1,0:T(2,128)(2,1)} %copy-done.15) | copy-start | bytes 49156
  389.0 691.1 %all-gather.7.cloned.1.call-start = ((), (), s32[]{:S(2)}) async-start(), calls=%async_computation.7 | async-start | bytes 2228224 | tf_op jit(solution)/shard_map/all_gather | solution.py:160
  389.5 686.5 %copy-start.4 = (bf16[1,512,1024]{2,1,0:T(8,128)(2,1)S(1)}, bf16[1,512,1024]{2,1,0:T(8,128)(2,1)}, u32[]{:S(2)}) copy-start(bf16[1,512,1024]{2,1,0:T(8,128)(2,1)} %all-gather.9.cloned.1.call-done) | copy-start | bytes 3145732
  517.5 623.5 %all-reduce.17.cloned.1.call-start = ((), (), s32[]{:S(2)}) async-start(), calls=%async_computation.12 | async-start | bytes 2228224 | tf_op jit(solution)/shard_map/psum | solution.py:183
  1080.1 101.2 %reduce-scatter.8.cloned.1.call-start = ((), (), s32[]{:S(2)}) async-start(), calls=%async_computation.9 | async-start | bytes 2359296 | tf_op jit(solution)/shard_map/reduce_scatter | solution.py:162
  1085.4 95.9 %copy-start.7 = (bf16[1,64,1024]{2,1,0:T(8,128)(2,1)S(1)}, bf16[1,64,1024]{2,1,0:T(8,128)(2,1)}, u32[]{:S(2)}) copy-start(bf16[1,64,1024]{2,1,0:T(8,128)(2,1)} %param.11) | copy-start | bytes 393220
  1085.4 95.9 %copy-start.21 = (f32[1024]{0:T(1024)S(1)}, f32[1024]{0:T(1024)}, u32[]{:S(2)}) copy-start(f32[1024]{0:T(1024)} %param.13) | copy-start | bytes 12292
  1085.4 95.9 %copy-start.25 = (f32[64]{0:T(128)S(1)}, f32[64]{0:T(128)}, u32[]{:S(2)}) copy-start(f32[64]{0:T(128)} %copy-done.24) | copy-start | bytes 772
  1085.5 128.5 %copy-start.11 = (bf16[1,64,1024]{2,1,0:T(8,128)(2,1)S(1)}, bf16[1,64,1024]{2,1,0:T(8,128)(2,1)}, u32[]{:S(2)}) copy-start(bf16[1,64,1024]{2,1,0:T(8,128)(2,1)} %param.12) | copy-start | bytes 393220
  1087.3 133.7 %all-reduce.15.cloned.1.call-start = ((), (), s32[]{:S(2)}) async-start(), calls=%async_computation.11 | async-start | bytes 131072 | tf_op jit(solution)/shard_map/psum | solution.py:183
  (12 other events, 225.7 us)
Sparse Core Ops, SparseCore 0:
  40.4 35.2 all-gather.4
  77.5 37.1 all-gather.8
  117.9 126.2 all-reduce.10
  246.7 67.0 reduce-scatter.3
  316.4 67.9 reduce-scatter.5
  389.1 124.6 all-reduce.12
  517.6 41.6 all-gather.6
  1080.2 60.7 all-reduce.16
  1143.7 37.5 reduce-scatter.7
  1184.5 36.4 all-reduce.14
where the time goes:
time: 1240 us; the launch traced here: 1230 us
  blocking collectives  670 us (54%)
  waiting for transfers between devices  480 us (39%)
  matrix products  43.7 us (4%)
  between operations  14.6 us (1%)
    psum x1, blocking collectives, local(): lax.psum(jnp.concatenate([back_q, back_k, back_v], axis=1), ('fsdp', 'ten...  549 us
    psum x1, waiting for transfers between devices, local(): kv_grads = lax.psum(jnp.stack([dkey, dval], axis=1), 'fsdp')  124 us
    reduce_scatter x1, waiting for transfers between devices, local(): lax.psum_scatter(contract_product(block, normed_hidden, 0, 1), 'fsdp', sc...  67.4 us
    reduce_scatter x1, waiting for transfers between devices, local(): lax.psum_scatter(contract_product(block, output_gradient, 1, 1), 'fsdp',...  66.8 us
    psum x1, waiting for transfers between devices, local(): keyvalue_total, low_sum = lax.psum((kv_part, lowrank_piece), 'fsdp')  60.7 us
    psum x1, blocking collectives, local(): backward_output = lax.psum(backward_piece, 'fsdp')  59.7 us
    psum x2, waiting for transfers between devices, local(): lax.psum((projection_down_gradient, query_up_gradient, keyvalue_up_gradie...  57.4 us
    reduce_scatter x1, waiting for transfers between devices, local(): lax.psum_scatter(contract_product(dq_group, qweight, 1, 1) + contract_pro...  38.8 us
  transfers between devices with their start and end apart: 10, of which 9 were waited for; matrix products, arithmetic and copies ran while one was open for 4% of the time, Pallas kernels for 0%

commit v1 on v0

v1 whole, which is shorter than its diff:
```python
import math

import jax
import jax.numpy as jnp
import numpy as np
from jax import lax
from jax.experimental import pallas as pl
from jax.experimental.pallas import tpu as pltpu
from jax.sharding import PartitionSpec as P

eps = 1e-05
adapter_scale = 2.0
theta = 500000.0
MESH = pl.DeviceIdType.MESH
F32 = jnp.float32
BF16 = jnp.bfloat16

NF = 16
NC = 8
NT = 8
L = 512
T = 64
W = 1024
H = 128
R = 32


def rope_tables():
    half = H // 2
    freq = np.float32(theta) ** (-(np.arange(half, dtype=np.float32) * np.float32(2.0)) / np.float32(H))
    angles = np.arange(L, dtype=np.float32)[:, None] * freq[None, :].astype(np.float32)
    angles = angles.astype(np.float64)
    cosine, sine = np.cos(angles), np.sin(angles)
    return (
        np.concatenate([cosine, cosine], axis=1).astype(np.float32),
        np.concatenate([-sine, sine], axis=1).astype(np.float32),
    )


def dot(a, b, ca, cb, **kw):
    return lax.dot_general(a, b, (((ca,), (cb,)), ((), ())), preferred_element_type=F32, **kw)


def rotate(v, c, s):
    return v * c + pltpu.roll(v, H // 2, axis=1) * s


def rotate_back(v, c, s):
    return v * c - pltpu.roll(v, H // 2, axis=1) * s


def kernel(
    x_h, g_h, gain_h, wq_h, wo_h, wkv_h, dwt_h, gup_h, ups_h, odt_h, cos_h, sin_h,
    hid_o, pd_o, ou_o, sm_o,
    xb, gb, nb, wq, wo, wkv, dwt, gup, upq, upk, upv, odt, odb, gain, cosb, sinb,
    ss_own, ss_recv, r_all, ip_own, ip_recv,
    bo_part, bo_recv, bo_all, kvl_part, kvl_recv, kvl_all,
    a_acc, a_pair, a_precv, a_send, a_recv,
    q_acc, q_pair, q_precv, q_send, q_recv,
    dq_all, qrot, dat, attn, dkacc,
    p1_part, p1_recv, dkv_all, p2_all, back_all,
    zpart, rs_sendr, rs_recvr, rs_sendl, rs_recvl,
    sm_own, sm_recv, sl_own, sl_recv, sl_all,
    ld, grp_s, grp_r, ring_s, ring_r, pair_s, pair_r, chip_s, chip_r, rs_s, rs_r, dp_s, dp_r,
):
    d = lax.axis_index("dp")
    f = lax.axis_index("fsdp")
    t = lax.axis_index("tensor")
    c = f // 2
    k = f % 2

    def rcopy(src, dst, ss, rs, dev):
        return pltpu.make_async_remote_copy(
            src_ref=src, dst_ref=dst, send_sem=ss, recv_sem=rs, device_id=dev, device_id_type=MESH
        )

    def wait_bytes(ref, sem):
        pltpu.make_async_copy(ref, ref, sem).wait()

    def fdev(i):
        return (d, lax.rem(f + i, NF), t)

    def zdev(i):
        return (d, f, lax.rem(t + i + NT, NT))

    loads = [
        (x_h, xb.at[pl.ds(pl.multiple_of(t * T, T), T)]),
        (g_h, gb.at[pl.ds(pl.multiple_of(t * T, T), T)]),
        (gain_h, gain),
        (wo_h, wo),
        (wq_h, wq),
        (wkv_h, wkv),
        (dwt_h, dwt.at[pl.ds(0, 192)]),
        (gup_h, gup.at[pl.ds(0, 64)]),
        (ups_h.at[pl.ds(0, 64)], upq.at[pl.ds(0, 64)]),
        (ups_h.at[pl.ds(64, 64)], upk.at[pl.ds(64, 64)]),
        (ups_h.at[pl.ds(128, 64)], upv.at[pl.ds(128, 64)]),
        (odt_h, odt.at[pl.ds(0, 64)]),
        (odt_h, odb.at[pl.ds(192, 64)]),
        (cos_h, cosb),
        (sin_h, sinb),
    ]
    copies = [pltpu.make_async_copy(s, o, ld.at[i]) for i, (s, o) in enumerate(loads)]
    for copy in copies:
        copy.start()

    barrier = pltpu.get_barrier_semaphore()

    @pl.loop(1, NF)
    def _(i):
        pl.semaphore_signal(barrier, inc=1, device_id=fdev(i), device_id_type=MESH)

    @pl.loop(1, NT)
    def _(i):
        pl.semaphore_signal(barrier, inc=1, device_id=zdev(i), device_id_type=MESH)

    other = (1 - d, f, t)
    pl.semaphore_signal(barrier, inc=1, device_id=other, device_id_type=MESH)

    dwt[pl.ds(192, 64)] = jnp.zeros((64, W), BF16)
    gup[pl.ds(64, 64)] = jnp.zeros((64, W), BF16)
    upq[pl.ds(64, 192)] = jnp.zeros((192, H), BF16)
    upk[pl.ds(0, 64)] = jnp.zeros((64, H), BF16)
    upk[pl.ds(128, 128)] = jnp.zeros((128, H), BF16)
    upv[pl.ds(0, 128)] = jnp.zeros((128, H), BF16)
    upv[pl.ds(192, 64)] = jnp.zeros((64, H), BF16)
    odt[pl.ds(64, 64)] = jnp.zeros((64, H), BF16)
    odb[pl.ds(0, 192)] = jnp.zeros((192, H), BF16)

    pl.semaphore_wait(barrier, NF - 1 + NT - 1 + 1)

    def ring(buf, rows, n):
        def piece(z, off, size):
            return buf.at[pl.ds(pl.multiple_of(lax.rem(t + z + 2 * NT, NT) * rows + off, 16), size)]

        def right(s):
            ref = piece(1 - s, 0, rows if s < 4 else rows // 2)
            return rcopy(ref, ref, ring_s.at[n, 0, s - 1], ring_r.at[n, 0, s - 1], zdev(1))

        def left(s):
            ref = piece(s - 1, 0, rows) if s < 4 else piece(3, rows // 2, rows // 2)
            return rcopy(ref, ref, ring_s.at[n, 1, s - 1], ring_r.at[n, 1, s - 1], zdev(-1))

        def start(s):
            right(s).start()
            left(s).start()

        def arrive(s):
            right(s).wait_recv()
            left(s).wait_recv()

        def finish():
            for s in range(1, 5):
                right(s).wait_send()
                left(s).wait_send()

        return start, arrive, finish

    g_start, g_arrive, g_finish = ring(gb, T, 0)
    x_start, x_arrive, x_finish = ring(xb, T, 1)
    sl_start, sl_arrive, sl_finish = ring(sl_all, 256, 2)

    def scatter_f(src, rows, recv, n):
        @pl.loop(1, NF)
        def _(i):
            fi = lax.rem(f + i, NF)
            rcopy(
                src.at[pl.ds(pl.multiple_of(fi * rows, rows), rows)],
                recv.at[i - 1],
                grp_s.at[n],
                grp_r.at[n],
                (d, fi, t),
            ).start()

    def gather_f(buf, rows, n):
        ref = buf.at[pl.ds(pl.multiple_of(f * rows, rows), rows)]

        @pl.loop(1, NF)
        def _(i):
            rcopy(ref, ref, grp_s.at[n], grp_r.at[n], fdev(i)).start()

    def total_f(own, recv):
        def add(i, total):
            return total + recv[i].astype(F32)

        return lax.fori_loop(0, NF - 1, add, own.astype(F32))

    copies[1].wait()
    g_start(1)
    copies[0].wait()

    own_rows = pl.ds(pl.multiple_of(t * T, T), T)
    ones = jnp.ones((8, W), F32)

    def column(rows8):
        return rows8.T[:T, 0:1]

    x_own = xb[own_rows].astype(F32)
    squares = dot(ones, x_own * x_own, 1, 1, precision=lax.Precision.HIGHEST)
    ss_own[...] = jnp.concatenate([squares, squares], axis=1)

    @pl.loop(1, NF)
    def _(i):
        rcopy(ss_own, ss_recv.at[i - 1], grp_s.at[0], grp_r.at[0], fdev(i)).start()

    g_arrive(1)
    g_start(2)
    x_start(1)
    wait_bytes(ss_recv, grp_r.at[0])
    squares = total_f(ss_own[...], ss_recv)
    r_all[t] = lax.rsqrt(squares / (W * NF) + eps)

    @pl.loop(1, NT)
    def _(i):
        rcopy(r_all.at[t], r_all.at[t], grp_s.at[1], grp_r.at[1], zdev(i)).start()

    copies[2].wait()

    def normalise(z):
        z = lax.rem(t + z + NT, NT)
        rows = pl.ds(pl.multiple_of(z * T, T), T)
        nb[rows] = (xb[rows].astype(F32) * column(r_all[z]) * gain[...]).astype(BF16)

    g_arrive(2)
    g_start(3)
    g_arrive(3)
    g_start(4)
    wait_bytes(r_all.at[pl.ds(0, NT - 1)], grp_r.at[1])
    normalise(0)
    copies[3].wait()
    copies[7].wait()
    g_arrive(4)

    bo_part[...] = dot(gb[...], gup[...], 1, 1).astype(BF16)
    scatter_f(bo_part, R, bo_recv, 2)

    mate = (d, 2 * c + 1 - k, t)

    def chip_at(i):
        return lax.rem(c + 1 + i, NC)

    def heads(product, acc, pair, precv, send, recv, n, extra):
        def pair_copy(i):
            return rcopy(pair.at[i], precv.at[i], pair_s.at[n, i], pair_r.at[n, i], mate)

        def chip_copy(i):
            dev = (d, 2 * chip_at(i) + k, t)
            return rcopy(send.at[i], recv.at[i], chip_s.at[n, i], chip_r.at[n, i], dev)

        def second(i):
            pair_copy(i).wait_recv()
            send[i] = (acc[i] + precv[i].astype(F32)).astype(BF16)
            chip_copy(i).start()

        @pl.loop(0, NC)
        def _(i):
            both = product(chip_at(i))
            acc[i] = jnp.where(k == 0, both[:, :H], both[:, H:])
            pair[i] = jnp.where(k == 0, both[:, H:], both[:, :H]).astype(BF16)
            pair_copy(i).start()

            @pl.when(i > 0)
            def _():
                second(i - 1)

            extra(i)

        pair_copy(NC - 1).wait_recv()

        def total():
            def add(i, value):
                chip_copy(i).wait_recv()
                return value + recv[i].astype(F32)

            return lax.fori_loop(0, NC - 1, add, acc[NC - 1] + precv[NC - 1].astype(F32))

        def finish():
            @pl.loop(0, NC)
            def _(i):
                pair_copy(i).wait_send()

            @pl.loop(0, NC - 1)
            def _(i):
                chip_copy(i).wait_send()

        return total, finish

    def a_product(ci):
        return dot(gb[...], wo[pl.ds(pl.multiple_of(ci * 256, 256), 256), :], 1, 1)

    def a_extra(i):
        for s in range(1, 4):

            @pl.when(i == 2 * s - 1)
            def _(s=s):
                x_arrive(s)
                x_start(s + 1)
                normalise(-s)
                normalise(s)

    a_total, a_finish = heads(a_product, a_acc, a_pair, a_precv, a_send, a_recv, 0, a_extra)

    wait_bytes(bo_recv, grp_r.at[2])
    own_piece = pl.ds(pl.multiple_of(f * R, R), R)
    bo_all[own_piece] = total_f(bo_part[own_piece], bo_recv).astype(BF16)
    gather_f(bo_all, R, 3)

    x_arrive(4)
    normalise(4)

    copies[5].wait()
    copies[6].wait()

    @pl.loop(0, 4)
    def _(i):
        rows = pl.ds(pl.multiple_of(i * 128, 128), 128)
        kvl_part[rows, pl.ds(0, 256)] = dot(nb[rows], wkv[...], 1, 0).astype(BF16)
        kvl_part[rows, pl.ds(256, 256)] = dot(nb[rows], dwt[...], 1, 1).astype(BF16)

    scatter_f(kvl_part, R, kvl_recv, 4)
    copies[4].wait()
    for i in range(8, 15):
        copies[i].wait()

    def q_product(ci):
        return dot(nb[...], wq[:, pl.ds(pl.multiple_of(ci * 256, 256), 256)], 1, 0)

    def q_extra(i):
        @pl.when(i == 4)
        def _():
            wait_bytes(kvl_recv, grp_r.at[4])
            total = total_f(kvl_part[own_piece], kvl_recv)
            low = total[:, 256:].astype(BF16)
            keys = total[:, :H] + adapter_scale * dot(low, upk[...], 1, 0)
            values = total[:, H:256] + adapter_scale * dot(low, upv[...], 1, 0)
            keys = rotate(keys, cosb[own_piece], sinb[own_piece])
            kvl_all[own_piece, pl.ds(0, H)] = keys.astype(BF16)
            kvl_all[own_piece, pl.ds(H, H)] = values.astype(BF16)
            kvl_all[own_piece, pl.ds(256, 256)] = low
            gather_f(kvl_all, R, 5)

    q_total, q_finish = heads(q_product, q_acc, q_pair, q_precv, q_send, q_recv, 1, q_extra)

    gathered = pl.ds(0, (NF - 1) * R)
    wait_bytes(bo_all.at[gathered], grp_r.at[3])
    dat[...] = (a_total() + adapter_scale * dot(bo_all[...], odt[...], 1, 0)).astype(BF16)

    wait_bytes(kvl_all.at[gathered], grp_r.at[5])
    low_cols = pl.ds(256, 256)
    query = q_total() + adapter_scale * dot(kvl_all[:, low_cols], upq[...], 1, 0)
    qrot[...] = rotate(query, cosb[...], sinb[...]).astype(BF16)

    scale = 1.0 / math.sqrt(H)
    dkacc[...] = jnp.zeros_like(dkacc)
    dq_cols = pl.ds(pl.multiple_of(f * H, H), H)
    for i in range(4):
        rows = pl.ds(i * 128, 128)
        seen = pl.ds(0, (i + 1) * 128)
        n = (i + 1) * 128
        krot = kvl_all[seen, pl.ds(0, H)]
        vals = kvl_all[seen, pl.ds(H, H)]
        qi = qrot[rows]
        da = dat[rows]
        scores = dot(qi, krot, 1, 1) * scale
        causal = lax.broadcasted_iota(jnp.int32, (128, n), 0) + i * 128 >= lax.broadcasted_iota(
            jnp.int32, (128, n), 1
        )
        scores = jnp.where(causal, scores, -1e30)
        e = jnp.exp(scores - jnp.max(scores, axis=1, keepdims=True))
        probs = e / jnp.sum(e, axis=1, keepdims=True)
        probs_b = probs.astype(BF16)
        attn[rows] = dot(probs_b, vals, 1, 0).astype(BF16)
        dprobs = dot(da, vals, 1, 1)
        delta = jnp.sum(probs * dprobs, axis=1, keepdims=True)
        dscore = (probs * (dprobs - delta) * scale).astype(BF16)
        dquery = dot(dscore, krot, 1, 0)
        dq_all[rows, dq_cols] = rotate_back(dquery, cosb[rows], sinb[rows]).astype(BF16)
        dkacc[seen, pl.ds(0, H)] += dot(dscore, qi, 0, 0)
        dkacc[seen, pl.ds(H, H)] += dot(probs_b, da, 0, 0)

    def dq_ref(ci, core):
        return dq_all.at[:, pl.ds(pl.multiple_of((2 * ci + core) * H, H), H)]

    def dq_copy(i):
        ref = dq_ref(c, k)
        return rcopy(ref, ref, chip_s.at[2, i], chip_r.at[2, i], (d, 2 * chip_at(i) + k, t))

    def dq_forward(i):
        ref = dq_ref(lax.rem(c - 1 - i + 2 * NC, NC), k)
        return rcopy(ref, ref, pair_s.at[2, i + 1], pair_r.at[2, i + 1], mate)

    @pl.loop(0, NC - 1)
    def _(i):
        dq_copy(i).start()

    dq_forward(-1).start()

    dq_own = dq_all[:, dq_cols]
    p1_part[:, pl.ds(0, 256)] = dkacc[...].astype(BF16)
    p1_part[:, pl.ds(256, 256)] = (
        dot(dq_own, upq[...], 1, 1) + dot(attn[...], odb[...], 1, 1)
    ).astype(BF16)
    scatter_f(p1_part, R, p1_recv, 6)

    sm_own[pl.ds(0, 64)] = dot(kvl_all[:, low_cols], dq_own, 0, 0)[:64]
    sm_own[pl.ds(192, 64)] = dot(bo_all[...], attn[...], 0, 0)[:64]

    wait_bytes(p1_recv, grp_r.at[6])
    total = total_f(p1_part[own_piece], p1_recv)
    dkey = rotate_back(total[:, :H], cosb[own_piece], sinb[own_piece]).astype(BF16)
    dval = total[:, H:256].astype(BF16)
    dkv_all[own_piece, pl.ds(0, H)] = dkey
    dkv_all[own_piece, pl.ds(H, H)] = dval
    gather_f(dkv_all, R, 7)
    p2_all[t] = (total[:, 256:] + dot(dkey, upk[...], 1, 1) + dot(dval, upv[...], 1, 1)).astype(BF16)

    @pl.loop(1, NT)
    def _(i):
        rcopy(p2_all.at[t], p2_all.at[t], grp_s.at[8], grp_r.at[8], zdev(i)).start()

    @pl.loop(0, NC - 1)
    def _(i):
        dq_copy(i).wait_recv()
        dq_forward(i).start()

    wait_bytes(p2_all.at[pl.ds(0, NT - 1)], grp_r.at[8])
    total = p2_all[0].astype(F32)
    for i in range(1, NT):
        total = total + p2_all[i].astype(F32)
    back_all[own_piece] = total.astype(BF16)
    gather_f(back_all, R, 9)

    wait_bytes(dkv_all.at[gathered], grp_r.at[7])
    kv_up = dot(kvl_all[:, low_cols], dkv_all[...], 0, 0)
    sm_own[pl.ds(64, 64)] = kv_up[64:128, :H]
    sm_own[pl.ds(128, 64)] = kv_up[128:192, H:]
    small = rcopy(sm_own, sm_recv, dp_s.at[0], dp_r.at[0], other)
    small.start()

    @pl.loop(0, NC)
    def _(i):
        dq_forward(i - 1).wait_recv()

    def depth(j, way):
        return 4 if j % 2 == way else 3

    def rs_copy(j, way, s):
        send, recv = ((rs_sendr, rs_recvr), (rs_sendl, rs_recvl))[way]
        return rcopy(
            send.at[j, s - 1], recv.at[j, s - 1], rs_s.at[way, j, s - 1], rs_r.at[way, j, s - 1], zdev(1 - 2 * way)
        )

    def rs_step(j, way, s):
        hops = depth(j, way) - s + 1
        z = lax.rem(t + (hops if way == 0 else -hops) + NT, NT)
        value = zpart[j, pl.ds(pl.multiple_of(z * T, T), T)]
        send, recv = ((rs_sendr, rs_recvr), (rs_sendl, rs_recvl))[way]
        if s > 1:
            rs_copy(j, way, s - 1).wait_recv()
            value = value + recv[j, s - 2].astype(F32)
        send[j, s - 1] = value.astype(BF16)
        rs_copy(j, way, s).start()

    for w in range(4 + 3):
        if w < 4:
            rows = pl.ds(w * 256, 256)
            zpart[w] = dot(dq_all[...], wq[rows, :], 1, 1) + dot(dkv_all[...], wkv[rows, :], 1, 1)
        for j in range(min(w, 3), -1, -1):
            s = w - j + 1
            for way in range(2):
                if s <= depth(j, way):
                    rs_step(j, way, s)

    wait_bytes(back_all.at[gathered], grp_r.at[9])
    cols = pl.ds(pl.multiple_of(t * H, H), H)
    sl_own[pl.ds(0, 192)] = dot(back_all[...], nb[:, cols], 0, 0)[:192]
    sl_own[pl.ds(192, 64)] = dot(back_all[...], gb[:, cols], 0, 0)[192:]
    slices = rcopy(sl_own, sl_recv, dp_s.at[1], dp_r.at[1], other)
    slices.start()

    back_own = back_all[own_rows]
    inverse = column(r_all[t])
    xhat = x_own * inverse
    dhat = []
    for j in range(4):
        wide = pl.ds(j * 256, 256)
        for way in range(2):
            rs_copy(j, way, depth(j, way)).wait_recv()
        value = zpart[j, own_rows] + rs_recvr[j, depth(j, 0) - 1].astype(F32) + rs_recvl[j, depth(j, 1) - 1].astype(F32)
        value = value + adapter_scale * dot(back_own, dwt[:, wide], 1, 0)
        dhat.append(value * gain[:, wide])
    dhat = jnp.concatenate(dhat, axis=1)
    inner = dot(ones, dhat * xhat, 1, 1, precision=lax.Precision.HIGHEST)
    ip_own[...] = jnp.concatenate([inner, inner], axis=1)

    @pl.loop(1, NF)
    def _(i):
        rcopy(ip_own, ip_recv.at[i - 1], grp_s.at[10], grp_r.at[10], fdev(i)).start()

    slices.wait_recv()
    sl_all[pl.ds(pl.multiple_of(t * 256, 256), 256)] = (sl_own[...] + sl_recv[...]).astype(BF16)
    sl_start(1)

    small.wait_recv()
    sm_o[...] = sm_own[...] + sm_recv[...]

    wait_bytes(ip_recv, grp_r.at[10])
    inner = total_f(ip_own[...], ip_recv) / (W * NF)
    hid_o[...] = inverse * (dhat - xhat * column(inner))

    for s in range(1, 5):
        sl_arrive(s)
        if s < 4:
            sl_start(s + 1)
    for z in range(NT):
        piece = sl_all[pl.ds(z * 256, 256)].astype(F32)
        pd_o[:, pl.ds(z * H, H)] = piece[:192]
        ou_o[:, pl.ds(z * H, H)] = piece[192:]

    g_finish()
    x_finish()
    sl_finish()
    a_finish()
    q_finish()

    @pl.loop(0, NC - 1)
    def _(i):
        dq_copy(i).wait_send()

    @pl.loop(0, NC)
    def _(i):
        dq_forward(i - 1).wait_send()

    for j in range(4):
        for way in range(2):
            for s in range(1, depth(j, way) + 1):
                rs_copy(j, way, s).wait_send()
    small.wait_send()
    slices.wait_send()
    sent = [
        ss_recv, r_all.at[pl.ds(0, NT - 1)], bo_recv, bo_all.at[gathered], kvl_recv, kvl_all.at[gathered],
        p1_recv, dkv_all.at[gathered], p2_all.at[pl.ds(0, NT - 1)], back_all.at[gathered], ip_recv,
    ]
    for n, ref in enumerate(sent):
        wait_bytes(ref, grp_s.at[n])


def local(
    residual_input,
    block_output_gradient,
    norm_gain_vector,
    query_matrix,
    keyvalue_matrix,
    output_matrix,
    adapter_projection_down,
    adapter_query_up,
    adapter_keyvalue_up,
    adapter_output_down,
    adapter_output_up,
):
    cosine, sine = rope_tables()
    ups = jnp.concatenate(
        [adapter_query_up[:, 0, :], adapter_keyvalue_up[:, 0, :], adapter_keyvalue_up[:, 1, :]], axis=0
    )
    vm = pltpu.VMEM
    dma = pltpu.SemaphoreType.DMA
    chips = [
        vm((NC, L, H), F32),
        vm((NC, L, H), BF16),
        vm((NC, L, H), BF16),
        vm((NC - 1, L, H), BF16),
        vm((NC - 1, L, H), BF16),
    ]
    scratch = [
        vm((L, W), BF16), vm((L, W), BF16), vm((L, W), BF16),
        vm((W, 2048), BF16), vm((2048, W), BF16), vm((W, 256), BF16), vm((256, W), BF16), vm((128, W), BF16),
        vm((256, H), BF16), vm((256, H), BF16), vm((256, H), BF16), vm((128, H), BF16), vm((256, H), BF16),
        vm((1, W), F32), vm((L, H), F32), vm((L, H), F32),
        vm((8, H), F32), vm((NF - 1, 8, H), F32), vm((NT, 8, H), F32), vm((8, H), F32), vm((NF - 1, 8, H), F32),
        vm((L, H), BF16), vm((NF - 1, R, H), BF16), vm((L, H), BF16),
        vm((L, 512), BF16), vm((NF - 1, R, 512), BF16), vm((L, 512), BF16),
        *chips, *chips,
        vm((L, 2048), BF16), vm((L, H), BF16), vm((L, H), BF16), vm((L, H), BF16), vm((L, 256), F32),
        vm((L, 512), BF16), vm((NF - 1, R, 512), BF16), vm((L, 256), BF16), vm((NT, R, 256), BF16), vm((L, 256), BF16),
        vm((4, L, 256), F32),
        vm((4, 4, T, 256), BF16), vm((4, 4, T, 256), BF16), vm((4, 4, T, 256), BF16), vm((4, 4, T, 256), BF16),
        vm((256, H), F32), vm((256, H), F32), vm((256, H), F32), vm((256, H), F32), vm((NT * 256, H), BF16),
        dma((15,)), dma((11,)), dma((11,)), dma((3, 2, 4)), dma((3, 2, 4)),
        dma((3, NC)), dma((3, NC)), dma((3, NC)), dma((3, NC)), dma((2, 4, 4)), dma((2, 4, 4)),
        dma((2,)), dma((2,)),
    ]
    hidden, down, up, small = pl.pallas_call(
        kernel,
        out_shape=(
            jax.ShapeDtypeStruct((T, W), F32),
            jax.ShapeDtypeStruct((192, W), F32),
            jax.ShapeDtypeStruct((64, W), F32),
            jax.ShapeDtypeStruct((256, H), F32),
        ),
        in_specs=[pl.BlockSpec(memory_space=pl.ANY)] * 12,
        out_specs=(pl.BlockSpec(memory_space=pltpu.VMEM),) * 4,
        scratch_shapes=scratch,
        compiler_params=pltpu.CompilerParams(
            collective_id=0, has_side_effects=True, vmem_limit_bytes=60 * 2**20
        ),
        name="adapter_backward",
    )(
        residual_input[0],
        block_output_gradient[0],
        norm_gain_vector[None],
        query_matrix[:, 0, :],
        output_matrix[0],
        keyvalue_matrix.reshape(W, 256),
        adapter_projection_down.T,
        adapter_output_up,
        ups,
        adapter_output_down[0].T,
        jnp.asarray(cosine),
        jnp.asarray(sine),
    )
    hidden = block_output_gradient.astype(F32) + hidden[None]
    small = small * adapter_scale
    return (
        hidden,
        (down * adapter_scale).T,
        small[:64, None, :],
        jnp.stack([small[64:128], small[128:192]], axis=1),
        small[192:].T[None],
        up * adapter_scale,
    )


def solution(mesh):
    in_specs = (
        P("dp", "tensor", "fsdp"),
        P("dp", "tensor", "fsdp"),
        P("fsdp"),
        P("fsdp", "tensor", None),
        P("fsdp", None, "tensor"),
        P("tensor", None, "fsdp"),
        P("fsdp", None),
        P(None, "tensor", "fsdp"),
        P(None, None, "tensor"),
        P("tensor", "fsdp", None),
        P(None, "fsdp"),
    )
    out_specs = (
        P("dp", "tensor", "fsdp"),
        P("fsdp", None),
        P(None, "tensor", "fsdp"),
        P(None, None, "tensor"),
        P("tensor", "fsdp", None),
        P(None, "fsdp"),
    )
    return jax.shard_map(local, mesh=mesh, in_specs=in_specs, out_specs=out_specs, check_vma=False)
```

time: 1240 us -> 168 us (0.14)
  blocking collectives: 670 us -> 0 us
  waiting for transfers between devices: 480 us -> 0 us
  Pallas kernels: 2.62 us -> 152 us
  matrix products: 43.7 us -> 0 us
  between operations: 14.6 us -> 0.67 us
    psum x4 -> x0, blocking collectives: 670 us -> none  [the longest x1 549 us: local(): lax.psum(jnp.concatenate([back_q, back_k, back_v], axis=1), ('fsdp', 'ten...]
    psum x4 -> x0, waiting for transfers between devices: 242 us -> none  [the longest x1 124 us: local(): kv_grads = lax.psum(jnp.stack([dkey, dval], axis=1), 'fsdp')]
    reduce_scatter x3 -> x0, waiting for transfers between devices: 173 us -> none  [the longest x1 67.4 us: local(): lax.psum_scatter(contract_product(block, normed_hidden, 0, 1), 'fsdp', sc...]
    pallas_call x0 -> x1, Pallas kernels: none -> 152 us  [local(): pl.pallas_call(kernel, out_shape=(jax.ShapeDtypeStruct((T, W), F32), jax....]
    all_gather x3 -> x0, waiting for transfers between devices: 64.1 us -> none  [the longest x1 34.6 us: local(): normed_hidden = lax.all_gather(normed_shard, 'tensor', axis=0, tiled=True)]
    dot_general x27 -> x0, matrix products: 43.7 us -> none  [the longest x20 35.6 us: contract_product(): lax.dot_general(left, right, (((left_dim,), (right_dim,)), ((), ())), pre...]
  transfers between devices with their start and end apart: 10 -> 0, of which waited for: 9 -> 0; matrix products, arithmetic and copies ran while one was open for 4% -> 0% of each run, Pallas kernels for 0% -> 0%
where the time goes in v1:
time: 168 us; the launch traced here: 165 us
  Pallas kernels  152 us (90%)
  other arithmetic  7.71 us (5%)
  local copies, waits for them, and re-layouts  4.14 us (2%)
    pallas_call x1, Pallas kernels, local(): pl.pallas_call(kernel, out_shape=(jax.ShapeDtypeStruct((T, W), F32), jax....  152 us

profile of v1, /device:TPU:1, one launch (start us, length us, event | category | flops | bytes accessed | tf_op | source)
XLA Modules:
  0.0 164.7 jit_solution(14781903570306872887)
XLA Ops:
  0.6 0.9 fusion
  1.5 1.3 pad_maximum_fusion.1.ups_h
  2.9 1.9 %copy.29 = bf16[128,8,2,128]{3,1,2,0:T(8,128)(2,1)} copy(bf16[128,8,2,128]{3,2,1,0:T(2,128)(2,1)} %bitcast.37) | data formatting | bytes 1048576
  4.8 0.0 copy-start
  4.8 152.2 %adapter_backward.1 = (f32[64,1024]{1,0:T(8,128)}, f32[192,1024]{1,0:T(8,128)}, f32[64,1024]{1,0:T(8,128)}, f32[256,128]{1,0:T(8,128)}) custom-call(bf16[64,1024]{1,0:T(8,128)(2,1)} %bitcast.39, bf16[64,1024]{1,0:T(8,128)(2,1)} %bitcast.36, f32[1,1024]{1,0:T(1,128)} %bitcast.43, bf16[1024,2048]{1,0:T(8,128)(2,1)} %bitcast.33, bf16[2048,1024]{1,0:T(8,128)(2,1)} %bitcast.34, ...), custom_call_target="tpu_custom_call" | custom-call | tf_op jit(solution)/shard_map/adapter_backward/pallas_call | solution.py:592
  157.0 0.0 copy-done
  157.0 1.7 %bitcast_add_fusion = f32[1,64,1024]{2,1,0:T(8,128)} fusion(f32[64,1024]{1,0:T(8,128)} %get-tuple-element.10, bf16[1,64,1024]{2,1,0:T(8,128)(2,1)S(1)} %copy-done), kind=kLoop, calls=%fused_computation.2 | loop fusion | flops 131072 | bytes 655360 | tf_op jit(solution)/shard_map/add | solution.py:621
  158.7 0.9 broadcast_multiply_fusion.1
  159.6 0.6 slice_bitcast_fusion
  160.3 0.7 copy.22
  160.9 1.7 %broadcast_multiply_fusion = f32[64,1024]{1,0:T(8,128)} fusion(f32[64,1024]{1,0:T(8,128)} %get-tuple-element.13), kind=kLoop, calls=%fused_computation.3 | loop fusion | flops 65536 | bytes 524288 | tf_op jit(solution)/shard_map/mul | solution.py:629
  162.6 2.1 %multiply_bitcast_fusion = f32[1024,192]{0,1:T(8,128)} fusion(f32[192,1024]{1,0:T(8,128)} %get-tuple-element.11), kind=kLoop, calls=%fused_computation | loop fusion | flops 196608 | bytes 1572864 | tf_op jit(solution)/shard_map/transpose | solution.py:625
  (2 shorter events, 0.0 us)
Async XLA Ops:
  4.8 152.2 %copy-start = (bf16[1,64,1024]{2,1,0:T(8,128)(2,1)S(1)}, bf16[1,64,1024]{2,1,0:T(8,128)(2,1)}, u32[]{:S(2)}) copy-start(bf16[1,64,1024]{2,1,0:T(8,128)(2,1)} %param.14) | copy-start | bytes 393220

commit v2 on v1

v2 whole, which is shorter than its diff:
```python
import math

import jax
import jax.numpy as jnp
import numpy as np
from jax import lax
from jax.experimental import pallas as pl
from jax.experimental.pallas import tpu as pltpu
from jax.sharding import PartitionSpec as P

eps = 1e-05
adapter_scale = 2.0
theta = 500000.0
MESH = pl.DeviceIdType.MESH
F32 = jnp.float32
BF16 = jnp.bfloat16

NF = 16
NC = 8
NT = 8
L = 512
T = 64
W = 1024
H = 128
R = 32


def rope_tables():
    half = H // 2
    freq = np.float32(theta) ** (-(np.arange(half, dtype=np.float32) * np.float32(2.0)) / np.float32(H))
    angles = np.arange(L, dtype=np.float32)[:, None] * freq[None, :].astype(np.float32)
    angles = angles.astype(np.float64)
    cosine, sine = np.cos(angles), np.sin(angles)
    return (
        np.concatenate([cosine, cosine], axis=1).astype(np.float32),
        np.concatenate([-sine, sine], axis=1).astype(np.float32),
    )


def dot(a, b, ca, cb, **kw):
    return lax.dot_general(a, b, (((ca,), (cb,)), ((), ())), preferred_element_type=F32, **kw)


def rotate(v, c, s):
    return v * c + pltpu.roll(v, H // 2, axis=1) * s


def rotate_back(v, c, s):
    return v * c - pltpu.roll(v, H // 2, axis=1) * s


def kernel(
    x_h, g_h, gain_h, wq_h, wo_h, wkv_h, dwt_h, gup_h, upq_h, upkv_h, odt_h, cos_h, sin_h,
    hid_o, pd_o, ou_o, sm_o,
    xb, gb, nb, wq, wo, wkv, dwt, gup, upq, upk, upv, odt, odb, gain, cosb, sinb, wkv_in, wkv_f, upkv_in, upkv_f,
    ss_own, ss_recv, r_all, ip_own, ip_recv, bo_part, bo_recv, bo_all,
    kvl_part, kvl_pair, kvl_send, kvl_recv, kvl_all,
    a_acc_o, a_acc_s, a_ps_o, a_ps_s, a_pr_o, a_pr_s, a_xs, a_xr, a_ys, a_yr,
    q_acc_o, q_acc_s, q_ps_o, q_ps_s, q_pr_o, q_pr_s, q_xs, q_xr, q_ys, q_yr,
    qrot, dat, attn, dq_own, dq_all, dkacc,
    p1_part, p1_pair, p1_send, p1_recv, dkv_all, dkv_slot, p2_all, back_all, back_slot,
    zpart, rs_sendr, rs_recvr, rs_sendl, rs_recvl, sm_own, sm_recv, ex_own, ex_recv,
    ld, grp_s, grp_r, ring_s, ring_r, kp_s, kp_r, pair_s, pair_r, xm_s, xm_r, yy_s, yy_r,
    dqy_s, dqy_r, dqx_s, dqx_r, dqc_s, dqc_r, rs_s, rs_r, dp_s, dp_r,
):
    d = lax.axis_index("dp")
    f = lax.axis_index("fsdp")
    t = lax.axis_index("tensor")
    c = f // 2
    k = f % 2
    xl = c // 4
    y = c % 4

    def rcopy(src, dst, ss, rs, dev):
        return pltpu.make_async_remote_copy(
            src_ref=src, dst_ref=dst, send_sem=ss, recv_sem=rs, device_id=dev, device_id_type=MESH
        )

    def wait_bytes(ref, sem):
        pltpu.make_async_copy(ref, ref, sem).wait()

    def fdev(i):
        return (d, lax.rem(f + i, NF), t)

    def zdev(i):
        return (d, f, lax.rem(t + i + NT, NT))

    mate = (d, 2 * c + 1 - k, t)
    xmate = (d, 2 * (4 * (1 - xl) + y) + k, t)
    other = (1 - d, f, t)

    def block(slot):
        rel = jnp.where(slot % 2 == 1, (slot + 1) // 2, NT - slot // 2) if not isinstance(slot, int) else (
            (slot + 1) // 2 if slot % 2 == 1 else NT - slot // 2
        )
        return lax.rem(t + rel, NT)

    def block_rows(slot):
        return pl.ds(pl.multiple_of(block(slot) * T, T), T)

    def slot_rows(slot):
        return pl.ds(slot * T, T)

    loads = [
        (g_h, gb.at[slot_rows(0)]),
        (x_h, xb.at[slot_rows(0)]),
        (gain_h, gain),
        (wo_h, wo),
        (wq_h, wq),
        (wkv_h, wkv_in),
        (dwt_h.at[pl.ds(0, 64)], dwt.at[pl.ds(0, 64)]),
        (dwt_h.at[pl.ds(64, 128)], dwt.at[pl.ds(128, 128)]),
        (gup_h, gup.at[pl.ds(0, 64)]),
        (upq_h, upq.at[pl.ds(0, 64)]),
        (upkv_h, upkv_in),
        (odt_h, odt.at[pl.ds(0, 64)]),
        (odt_h, odb.at[pl.ds(64, 64)]),
        (cos_h, cosb),
        (sin_h, sinb),
    ]
    copies = [pltpu.make_async_copy(s, o, ld.at[i]) for i, (s, o) in enumerate(loads)]
    for copy in copies:
        copy.start()

    barrier = pltpu.get_barrier_semaphore()

    @pl.loop(1, NF)
    def _(i):
        pl.semaphore_signal(barrier, inc=1, device_id=fdev(i), device_id_type=MESH)

    @pl.loop(1, NT)
    def _(i):
        pl.semaphore_signal(barrier, inc=1, device_id=zdev(i), device_id_type=MESH)

    pl.semaphore_signal(barrier, inc=1, device_id=other, device_id_type=MESH)

    dwt[pl.ds(64, 64)] = jnp.zeros((64, W), BF16)
    gup[pl.ds(64, 64)] = jnp.zeros((64, W), BF16)
    upq[pl.ds(64, 192)] = jnp.zeros((192, H), BF16)
    upk[pl.ds(0, 128)] = jnp.zeros((128, H), BF16)
    upk[pl.ds(192, 64)] = jnp.zeros((64, H), BF16)
    upv[pl.ds(0, 192)] = jnp.zeros((192, H), BF16)
    odt[pl.ds(64, 64)] = jnp.zeros((64, H), BF16)
    odb[pl.ds(0, 64)] = jnp.zeros((64, H), BF16)
    dkacc[...] = jnp.zeros_like(dkacc)
    copies[0].wait()
    copies[1].wait()
    x_own = xb[slot_rows(0)].astype(F32)
    ones = jnp.ones((8, W), F32)
    squares = dot(ones, x_own * x_own, 1, 1, precision=lax.Precision.HIGHEST)
    ss_own[...] = jnp.concatenate([squares, squares], axis=1)

    pl.semaphore_wait(barrier, NF - 1 + NT - 1 + 1)

    def ring(buf, n):
        def right(s):
            src, dst = (0, 2, 4, 6)[s - 1], (2, 4, 6, 7)[s - 1]
            size = T if s < 4 else T // 2
            return rcopy(
                buf.at[pl.ds(src * T, size)], buf.at[pl.ds(dst * T, size)],
                ring_s.at[n, 0, s - 1], ring_r.at[n, 0, s - 1], zdev(1),
            )

        def left(s):
            src, dst = (0, 1, 3, 5)[s - 1], (1, 3, 5, 7)[s - 1]
            size, off = (T, 0) if s < 4 else (T // 2, T // 2)
            return rcopy(
                buf.at[pl.ds(src * T + off, size)], buf.at[pl.ds(dst * T + off, size)],
                ring_s.at[n, 1, s - 1], ring_r.at[n, 1, s - 1], zdev(-1),
            )

        def start(s):
            right(s).start()
            left(s).start()

        def arrive(s):
            right(s).wait_recv()
            left(s).wait_recv()

        def finish(last=4):
            for s in range(1, last + 1):
                right(s).wait_send()
                left(s).wait_send()

        return start, arrive, finish

    g_start, g_arrive, g_finish = ring(gb, 0)
    x_start, x_arrive, x_finish = ring(xb, 1)

    def column(rows8):
        return rows8.T[:T, 0:1]

    def gain_row():
        return jnp.concatenate([gain[pl.ds(i, 1)] for i in range(8)], axis=1)

    def normalise(slot):
        rows = slot_rows(slot)
        nb[rows] = (xb[rows].astype(F32) * column(r_all[block(slot)]) * gain_row()).astype(BF16)

    def heads(product, chunks, n, bufs):
        acc_o, acc_s, ps_o, ps_s, pr_o, pr_s, xs, xr, ys, yr = bufs

        def rows_of(ch):
            return pl.ds(*chunks[ch])

        def pair_copy(ch, g):
            src, dst = ((ps_o, pr_o), (ps_s, pr_s))[g]
            return rcopy(src.at[:, rows_of(ch)], dst.at[:, rows_of(ch)], pair_s.at[n, ch, g], pair_r.at[n, ch, g], mate)

        def x_copy(ch):
            return rcopy(xs.at[:, rows_of(ch)], xr.at[:, rows_of(ch)], xm_s.at[n, ch], xm_r.at[n, ch], xmate)

        def y_copy(ch, j):
            yj = lax.rem(y + j, 4)
            return rcopy(
                ys.at[yj, rows_of(ch)], yr.at[j - 1, rows_of(ch)], yy_s.at[n, ch, j - 1], yy_r.at[n, ch, j - 1],
                (d, 2 * (4 * xl + yj) + k, t),
            )

        def first(ch, g):
            rows = rows_of(ch)
            acc, ps = ((acc_o, ps_o), (acc_s, ps_s))[g]
            base = 4 * (1 - xl) if g == 0 else 4 * xl

            @pl.loop(0, 4)
            def _(i):
                both = product(rows, base + i)
                acc[i, rows] = jnp.where(k == 0, both[:, :H], both[:, H:])
                ps[i, rows] = jnp.where(k == 0, both[:, H:], both[:, :H]).astype(BF16)

            pair_copy(ch, g).start()

        def second(ch):
            rows = rows_of(ch)
            pair_copy(ch, 0).wait_recv()

            @pl.loop(0, 4)
            def _(i):
                xs[i, rows] = (acc_o[i, rows] + pr_o[i, rows].astype(F32)).astype(BF16)

            x_copy(ch).start()

        def third(ch):
            rows = rows_of(ch)
            pair_copy(ch, 1).wait_recv()
            x_copy(ch).wait_recv()
            for j in range(1, 4):
                yj = lax.rem(y + j, 4)
                ys[yj, rows] = (acc_s[yj, rows] + pr_s[yj, rows].astype(F32) + xr[yj, rows].astype(F32)).astype(BF16)
                y_copy(ch, j).start()

        def total(ch):
            rows = rows_of(ch)
            value = acc_s[y, rows] + pr_s[y, rows].astype(F32) + xr[y, rows].astype(F32)
            for j in range(1, 4):
                y_copy(ch, j).wait_recv()
                value = value + yr[j - 1, rows].astype(F32)
            return value

        def finish():
            for ch in range(len(chunks)):
                pair_copy(ch, 0).wait_send()
                pair_copy(ch, 1).wait_send()
                x_copy(ch).wait_send()
                for j in range(1, 4):
                    y_copy(ch, j).wait_send()

        return first, second, third, total, finish

    def a_product(rows, ci):
        return dot(gb[rows], wo[pl.ds(pl.multiple_of(ci * 256, 256), 256), :], 1, 1)

    def q_product(rows, ci):
        return dot(nb[rows], wq[:, pl.ds(pl.multiple_of(ci * 256, 256), 256)], 1, 0)

    a_chunks = [(0, 64), (64, 128), (192, 128), (320, 192)]
    q_chunks = [(0, 192), (192, 128), (320, 128), (448, 64)]
    a1, a2, a3, a_total, a_finish = heads(
        a_product, a_chunks, 0, (a_acc_o, a_acc_s, a_ps_o, a_ps_s, a_pr_o, a_pr_s, a_xs, a_xr, a_ys, a_yr)
    )
    q1, q2, q3, q_total, q_finish = heads(
        q_product, q_chunks, 1, (q_acc_o, q_acc_s, q_ps_o, q_ps_s, q_pr_o, q_pr_s, q_xs, q_xr, q_ys, q_yr)
    )

    def kvl_copy(ch):
        s0, n = q_chunks[ch][0] // T, q_chunks[ch][1] // T
        return rcopy(
            kvl_part.at[pl.ds(s0, n), 1 - k], kvl_pair.at[pl.ds(s0, n)], kp_s.at[ch], kp_r.at[ch], mate
        )

    def kvl1(ch):
        s0, n = q_chunks[ch][0] // T, q_chunks[ch][1] // T
        rows = pl.ds(*q_chunks[ch])
        kvl_part[pl.ds(s0, n), :, :, pl.ds(0, 256)] = dot(nb[rows], wkv[...], 1, 0).reshape(n, 2, R, 256)
        kvl_part[pl.ds(s0, n), :, :, pl.ds(256, 256)] = dot(nb[rows], dwt[...], 1, 1).reshape(n, 2, R, 256)
        kvl_copy(ch).start()

    def to_chip(send, recv, s, n):
        @pl.when(s != c)
        def _():
            rcopy(send.at[s], recv.at[c], grp_s.at[n], grp_r.at[n], (d, 2 * s + k, t)).start()

    def kvl2(ch):
        s0, n = q_chunks[ch][0] // T, q_chunks[ch][1] // T
        kvl_copy(ch).wait_recv()
        for s in range(s0, s0 + n):
            kvl_send[s] = kvl_part[s, k] + kvl_pair[s]
            to_chip(kvl_send, kvl_recv, s, 5)

    def chip_total(own, recv):
        def add(i, total):
            return total + recv[lax.rem(c + i, NC)].astype(F32)

        return lax.fori_loop(1, NC, add, own)

    def gather_chips(buf, z, n):
        ref = buf.at[z, k]

        @pl.loop(1, NC)
        def _(i):
            rcopy(ref, ref, grp_s.at[n], grp_r.at[n], (d, 2 * lax.rem(c + i, NC) + k, t)).start()

    def gather_mate(buf, n):
        return rcopy(buf.at[:, k], buf.at[:, k], grp_s.at[n], grp_r.at[n], mate)

    def seven(buf):
        return buf.at[pl.ds(0, NC - 1), 0]

    def total_f(own, recv):
        def add(i, total):
            return total + recv[i].astype(F32)

        return lax.fori_loop(0, NF - 1, add, own.astype(F32))

    g_start(1)
    x_start(1)

    @pl.loop(1, NF)
    def _(i):
        rcopy(ss_own, ss_recv.at[i - 1], grp_s.at[0], grp_r.at[0], fdev(i)).start()

    copies[3].wait()
    a1(0, 0)
    a1(0, 1)
    a2(0)
    wait_bytes(ss_recv, grp_r.at[0])
    squares = total_f(ss_own[...], ss_recv)
    r_all[t] = lax.rsqrt(squares / (W * NF) + eps)

    @pl.loop(1, NT)
    def _(i):
        rcopy(r_all.at[t], r_all.at[t], grp_s.at[1], grp_r.at[1], zdev(i)).start()

    g_arrive(1)
    g_start(2)
    a1(1, 0)
    x_arrive(1)
    x_start(2)
    a1(1, 1)
    a2(1)
    a3(0)
    for i in (2, 4, 5, 6, 7, 8, 9, 10):
        copies[i].wait()
    wkv_f[...] = wkv_in[...].astype(F32)
    wkv[:, pl.ds(0, H)] = wkv_f[pl.ds(0, W, stride=2)].astype(BF16)
    wkv[:, pl.ds(H, H)] = wkv_f[pl.ds(1, W, stride=2)].astype(BF16)
    upkv_f[...] = upkv_in[...].astype(F32)
    upk[pl.ds(128, 64)] = upkv_f[pl.ds(0, 64, stride=2)].astype(BF16)
    upv[pl.ds(192, 64)] = upkv_f[pl.ds(1, 64, stride=2)].astype(BF16)
    g_arrive(2)
    g_start(3)
    wait_bytes(r_all.at[pl.ds(0, NT - 1)], grp_r.at[1])
    for slot in range(3):
        normalise(slot)
    kvl1(0)
    x_arrive(2)
    x_start(3)
    q1(0, 0)
    q1(0, 1)
    kvl2(0)
    q2(0)
    g_arrive(3)
    g_start(4)
    normalise(3)
    normalise(4)
    kvl1(1)
    a1(2, 0)
    a3(1)
    a1(2, 1)
    x_arrive(3)
    x_start(4)
    kvl2(1)
    q1(1, 0)
    a2(2)
    q3(0)
    q1(1, 1)
    q2(1)
    normalise(5)
    normalise(6)
    kvl1(2)
    q1(2, 0)
    g_arrive(4)
    bo_part[...] = dot(gb[...], gup[...], 1, 1).astype(BF16)

    @pl.loop(1, NF)
    def _(i):
        fi = lax.rem(f + i, NF)
        rcopy(
            bo_part.at[pl.ds(pl.multiple_of(fi * R, R), R)], bo_recv.at[i - 1], grp_s.at[2], grp_r.at[2], (d, fi, t)
        ).start()

    kvl2(2)
    x_arrive(4)
    normalise(7)
    kvl1(3)
    q1(2, 1)
    kvl2(3)
    q1(3, 0)
    q2(2)
    q1(3, 1)
    q2(3)
    q3(1)
    a3(2)
    z_own = block(c)
    own_slots = pl.ds(pl.multiple_of(f * R, R), R)
    own_rows = pl.ds(pl.multiple_of(z_own * T + k * R, R), R)
    for i in range(11, 15):
        copies[i].wait()
    wait_bytes(kvl_recv.at[pl.ds(0, NC - 1)], grp_r.at[5])
    total = chip_total(kvl_send[c], kvl_recv)
    low = total[:, 256:].astype(BF16)
    keys = total[:, :H] + adapter_scale * dot(low, upk[...], 1, 0)
    values = total[:, H:256] + adapter_scale * dot(low, upv[...], 1, 0)
    keys = rotate(keys, cosb[own_rows], sinb[own_rows])
    kvl_all[z_own, k, :, pl.ds(0, H)] = keys.astype(BF16)
    kvl_all[z_own, k, :, pl.ds(H, H)] = values.astype(BF16)
    kvl_all[z_own, k, :, pl.ds(256, 256)] = low
    gather_chips(kvl_all, z_own, 6)
    wait_bytes(bo_recv, grp_r.at[2])
    bo_all[own_rows] = total_f(bo_part[own_slots], bo_recv).astype(BF16)
    bo_ref = bo_all.at[own_rows]

    @pl.loop(1, NF)
    def _(i):
        rcopy(bo_ref, bo_ref, grp_s.at[3], grp_r.at[3], fdev(i)).start()

    a1(3, 0)
    q3(2)
    a2(3)
    q3(3)
    a1(3, 1)
    a3(3)
    wait_bytes(seven(kvl_all), grp_r.at[6])
    gather_mate(kvl_all, 7).start()

    def a_store(ch):
        value = a_total(ch)
        r0, size = a_chunks[ch]
        for s in range(r0 // T, (r0 + size) // T):
            part = value[s * T - r0 : (s + 1) * T - r0]
            rows = block_rows(s)
            dat[rows] = (part + adapter_scale * dot(bo_all[rows], odt[...], 1, 0)).astype(BF16)

    wait_bytes(bo_all.at[pl.ds(0, (NF - 1) * R)], grp_r.at[3])
    for ch in range(3):
        a_store(ch)
    gather_mate(kvl_all, 7).wait_recv()
    for ch, (r0, size) in enumerate(q_chunks):
        value = q_total(ch)
        for s in range(r0 // T, (r0 + size) // T):
            part = value[s * T - r0 : (s + 1) * T - r0]
            rows = block_rows(s)
            low = kvl_all[block(s), :, :, pl.ds(256, 256)].reshape(T, 256)
            query = part + adapter_scale * dot(low, upq[...], 1, 0)
            qrot[rows] = rotate(query, cosb[rows], sinb[rows]).astype(BF16)
    a_store(3)

    scale = 1.0 / math.sqrt(H)
    for i in range(4):
        rows = pl.ds(i * 128, 128)
        n = (i + 1) * 128
        seen = pl.ds(0, n)
        krot = kvl_all[pl.ds(0, n // T), :, :, pl.ds(0, H)].reshape(n, H)
        vals = kvl_all[pl.ds(0, n // T), :, :, pl.ds(H, H)].reshape(n, H)
        qi = qrot[rows]
        da = dat[rows]
        scores = dot(qi, krot, 1, 1) * scale
        causal = lax.broadcasted_iota(jnp.int32, (128, n), 0) + i * 128 >= lax.broadcasted_iota(
            jnp.int32, (128, n), 1
        )
        scores = jnp.where(causal, scores, -1e30)
        e = jnp.exp(scores - jnp.max(scores, axis=1, keepdims=True))
        probs = e / jnp.sum(e, axis=1, keepdims=True)
        probs_b = probs.astype(BF16)
        attn[rows] = dot(probs_b, vals, 1, 0).astype(BF16)
        dprobs = dot(da, vals, 1, 1)
        delta = jnp.sum(probs * dprobs, axis=1, keepdims=True)
        dscore = (probs * (dprobs - delta) * scale).astype(BF16)
        dquery = dot(dscore, krot, 1, 0)
        dq_own[rows] = rotate_back(dquery, cosb[rows], sinb[rows]).astype(BF16)
        dkacc[seen, pl.ds(0, H)] += dot(dscore, qi, 0, 0)
        dkacc[seen, pl.ds(H, H)] += dot(probs_b, da, 0, 0)

    z_chunks = [(448, 64), (320, 128), (192, 128), (0, 192)]

    def dqy_copy(ch, j):
        ref = dq_all.at[xl, y, k, pl.ds(*z_chunks[ch])]
        return rcopy(
            ref, ref, dqy_s.at[ch, j - 1], dqy_r.at[ch, j - 1], (d, 2 * (4 * xl + lax.rem(y + j, 4)) + k, t)
        )

    def dqx_copy(ch):
        ref = dq_all.at[xl, :, k, pl.ds(*z_chunks[ch])]
        return rcopy(ref, ref, dqx_s.at[ch], dqx_r.at[ch], xmate)

    def dqc_copy(ch, g):
        ref = dq_all.at[xl if g == 0 else 1 - xl, :, k, pl.ds(*z_chunks[ch])]
        return rcopy(ref, ref, dqc_s.at[ch, g], dqc_r.at[ch, g], mate)

    def dq_send(ch):
        r0, size = z_chunks[ch]
        for s in range(r0 // T, (r0 + size) // T):
            dq_all[xl, y, k, slot_rows(s)] = dq_own[block_rows(s)]
        for j in range(1, 4):
            dqy_copy(ch, j).start()

    def dq_forward_x(ch):
        for j in range(1, 4):
            dqy_copy(ch, j).wait_recv()
        dqx_copy(ch).start()
        dqc_copy(ch, 0).start()

    def dq_forward_core(ch):
        dqx_copy(ch).wait_recv()
        dqc_copy(ch, 1).start()

    dq_send(0)
    p1_part[:, :, :, pl.ds(0, 256)] = dkacc[...].reshape(NC, 2, R, 256)
    p1_part[:, :, :, pl.ds(256, H)] = (
        dot(dq_own[...], upq[pl.ds(0, H)], 1, 1) + dot(attn[...], odb[...], 1, 1)
    ).reshape(NC, 2, R, H)
    p1_copy = rcopy(p1_part.at[:, 1 - k], p1_pair, grp_s.at[8], grp_r.at[8], mate)
    p1_copy.start()
    sm_own[pl.ds(192, 64)] = dot(bo_all[...], attn[...], 0, 0)[:64]
    p1_copy.wait_recv()
    for s in range(NC):
        p1_send[s] = (p1_part[s, k] + p1_pair[s]).astype(BF16)
        to_chip(p1_send, p1_recv, s, 9)
    dq_send(1)
    all_low = kvl_all[:, :, :, pl.ds(256, 256)].reshape(L, 256)
    sm_own[pl.ds(0, 64)] = dot(all_low, dq_own[...], 0, 0)[:64]
    dq_forward_x(0)
    wait_bytes(p1_recv.at[pl.ds(0, NC - 1)], grp_r.at[9])
    total = chip_total(p1_part[c, k] + p1_pair[c], p1_recv)
    piece = pl.ds(pl.multiple_of(f * R, R), R)
    dkey = rotate_back(total[:, :H], cosb[piece], sinb[piece]).astype(BF16)
    dval = total[:, H:256].astype(BF16)
    dkv_all[c, k, :, pl.ds(0, H)] = dkey
    dkv_all[c, k, :, pl.ds(H, H)] = dval
    gather_chips(dkv_all, c, 10)
    p2_all[t, :, pl.ds(0, H)] = total[:, 256:].astype(BF16)
    p2_all[t, :, pl.ds(H, H)] = (
        dot(dkey, upk[pl.ds(H, H)], 1, 1) + dot(dval, upv[pl.ds(H, H)], 1, 1)
    ).astype(BF16)

    @pl.loop(1, NT)
    def _(i):
        rcopy(p2_all.at[t], p2_all.at[t], grp_s.at[12], grp_r.at[12], zdev(i)).start()

    dq_forward_core(0)
    dq_forward_x(1)
    dq_send(2)
    dq_send(3)
    wait_bytes(seven(dkv_all), grp_r.at[10])
    gather_mate(dkv_all, 11).start()
    wait_bytes(p2_all.at[pl.ds(0, NT - 1)], grp_r.at[12])
    total = p2_all[0].astype(F32)
    for i in range(1, NT):
        total = total + p2_all[i].astype(F32)
    back_all[c, k] = total.astype(BF16)
    gather_chips(back_all, c, 13)
    gather_mate(dkv_all, 11).wait_recv()
    for s in range(NT):
        dkv_slot[slot_rows(s)] = dkv_all[block(s)].reshape(T, 256)

    def slots_of(j, way):
        far = ([7, 5, 3, 1], [7, 6, 4, 2])[way]
        return far if j % 2 == way else far[1:]

    def rs_copy(j, way, s):
        send, recv = ((rs_sendr, rs_recvr), (rs_sendl, rs_recvl))[way]
        return rcopy(
            send.at[j, s], recv.at[j, s], rs_s.at[way, j, s], rs_r.at[way, j, s], zdev(1 - 2 * way)
        )

    def rs_step(j, way, s):
        value = zpart[j, slot_rows(slots_of(j, way)[s])]
        send, recv = ((rs_sendr, rs_recvr), (rs_sendl, rs_recvl))[way]
        if s > 0:
            rs_copy(j, way, s - 1).wait_recv()
            value = value + recv[j, s - 1].astype(F32)
        send[j, s] = value.astype(BF16)
        rs_copy(j, way, s).start()

    for ch in range(4):
        rows = pl.ds(*z_chunks[ch])
        if ch == 1:
            dq_forward_core(1)
            dq_forward_x(2)
        if ch == 2:
            dq_forward_core(2)
            dq_forward_x(3)
        if ch == 3:
            dq_forward_core(3)
        dqc_copy(ch, 0).wait_recv()
        dqc_copy(ch, 1).wait_recv()
        dq = jnp.concatenate([dq_all[i // 8, i // 2 % 4, i % 2, rows] for i in range(NF)], axis=1)
        for j in range(4):
            wide = pl.ds(j * 256, 256)
            zpart[j, rows] = dot(dq, wq[wide, :], 1, 1) + dot(dkv_slot[rows], wkv[wide, :], 1, 1)
            for way in range(2):
                s = ch if j % 2 == way else ch - 1
                if s >= 0:
                    rs_step(j, way, s)
        if ch == 1:
            wait_bytes(seven(back_all), grp_r.at[13])
            gather_mate(back_all, 14).start()

    gather_mate(back_all, 14).wait_recv()
    for s in range(NT):
        back_slot[slot_rows(s)] = back_all[block(s)].reshape(T, 256)
    halves = []
    for i in range(2):
        rows = pl.ds(i * 128, 128)
        ex_own[rows] = dot(back_slot[:, rows], nb[...], 0, 0).astype(BF16)
        if i == 0:
            ex_own[pl.ds(64, 64)] = dot(back_slot[:, rows], gb[...], 0, 0)[64:].astype(BF16)
        halves.append(rcopy(ex_own.at[rows], ex_recv.at[rows], dp_s.at[1 + i], dp_r.at[1 + i], other))
        halves[i].start()
    kv_up = dot(all_low, dkv_all[...].reshape(L, 256), 0, 0)
    sm_own[pl.ds(64, 64)] = kv_up[128:192, :H]
    sm_own[pl.ds(128, 64)] = kv_up[192:, H:]
    small = rcopy(sm_own, sm_recv, dp_s.at[0], dp_r.at[0], other)
    small.start()

    inverse = column(r_all[t])
    xhat = x_own * inverse
    dhat = []
    for j in range(4):
        wide = pl.ds(j * 256, 256)
        value = zpart[j, slot_rows(0)] + adapter_scale * dot(back_slot[slot_rows(0)], dwt[:, wide], 1, 0)
        for way, recv in enumerate((rs_recvr, rs_recvl)):
            last = len(slots_of(j, way)) - 1
            rs_copy(j, way, last).wait_recv()
            value = value + recv[j, last].astype(F32)
        dhat.append(value)
    dhat = jnp.concatenate(dhat, axis=1) * gain_row()
    inner = dot(ones, dhat * xhat, 1, 1, precision=lax.Precision.HIGHEST)
    ip_own[...] = jnp.concatenate([inner, inner], axis=1)

    @pl.loop(1, NF)
    def _(i):
        rcopy(ip_own, ip_recv.at[i - 1], grp_s.at[15], grp_r.at[15], fdev(i)).start()

    small.wait_recv()
    both = adapter_scale * (sm_own[...] + sm_recv[...])
    sm_o[pl.ds(0, 64)] = both[:64]
    sm_o[pl.ds(64, 64, stride=2)] = both[64:128]
    sm_o[pl.ds(65, 64, stride=2)] = both[128:192]
    sm_o[pl.ds(192, 64)] = both[192:]
    wait_bytes(ip_recv, grp_r.at[15])
    inner = total_f(ip_own[...], ip_recv) / (W * NF)
    hid_o[...] = gb[slot_rows(0)].astype(F32) + inverse * (dhat - xhat * column(inner))
    halves[0].wait_recv()

    def added(i, n):
        return adapter_scale * (ex_own[pl.ds(i, n)].astype(F32) + ex_recv[pl.ds(i, n)].astype(F32))

    pd_o[pl.ds(0, 64)] = added(0, 64)
    ou_o[...] = added(64, 64)
    halves[1].wait_recv()
    pd_o[pl.ds(64, 128)] = added(128, 128)

    g_finish()
    x_finish()
    a_finish()
    q_finish()
    for ch in range(4):
        kvl_copy(ch).wait_send()
        dqx_copy(ch).wait_send()
        dqc_copy(ch, 0).wait_send()
        dqc_copy(ch, 1).wait_send()
        for j in range(1, 4):
            dqy_copy(ch, j).wait_send()
    for j in range(4):
        for way in range(2):
            for s in range(len(slots_of(j, way))):
                rs_copy(j, way, s).wait_send()
    p1_copy.wait_send()
    small.wait_send()
    for half in halves:
        half.wait_send()
    gather_mate(kvl_all, 7).wait_send()
    gather_mate(dkv_all, 11).wait_send()
    gather_mate(back_all, 14).wait_send()
    sent = {
        0: ss_recv, 1: r_all.at[pl.ds(0, NT - 1)], 2: bo_recv, 3: bo_all.at[pl.ds(0, (NF - 1) * R)],
        5: kvl_recv.at[pl.ds(0, NC - 1)], 6: seven(kvl_all), 9: p1_recv.at[pl.ds(0, NC - 1)], 10: seven(dkv_all),
        12: p2_all.at[pl.ds(0, NT - 1)], 13: seven(back_all), 15: ip_recv,
    }
    for n, ref in sent.items():
        wait_bytes(ref, grp_s.at[n])


def hand_over(hid, pd, ou, sm, hid_o, pd_o, ou_o, qu_o, ku_o, od_o):
    hid_o[...] = hid[...]
    pd_o[...] = pd[...]
    ou_o[...] = ou[...]
    qu_o[...] = sm[pl.ds(0, 64)]
    ku_o[...] = sm[pl.ds(64, 128)]
    od_o[...] = sm[pl.ds(192, 64)]


def local(
    residual_input,
    block_output_gradient,
    norm_gain_vector,
    query_matrix,
    keyvalue_matrix,
    output_matrix,
    adapter_projection_down,
    adapter_query_up,
    adapter_keyvalue_up,
    adapter_output_down,
    adapter_output_up,
):
    cosine, sine = rope_tables()
    vm = pltpu.VMEM
    dma = pltpu.SemaphoreType.DMA
    quarter = [vm((4, L, H), BF16)] * 7 + [vm((3, L, H), BF16)]
    heads = [vm((4, L, H), F32)] * 2 + quarter
    scratch = [
        vm((L, W), BF16), vm((L, W), BF16), vm((L, W), BF16),
        vm((W, 2048), BF16), vm((2048, W), BF16), vm((W, 256), BF16), vm((256, W), BF16), vm((128, W), BF16),
        vm((256, H), BF16), vm((256, H), BF16), vm((256, H), BF16), vm((128, H), BF16), vm((128, H), BF16),
        vm((8, H), F32), vm((L, H), F32), vm((L, H), F32),
        vm((2 * W, H), BF16), vm((2 * W, H), F32), vm((128, H), BF16), vm((128, H), F32),
        vm((8, H), F32), vm((NF - 1, 8, H), F32), vm((NT, 8, H), F32), vm((8, H), F32), vm((NF - 1, 8, H), F32),
        vm((L, H), BF16), vm((NF - 1, R, H), BF16), vm((L, H), BF16),
        vm((NC, 2, R, 512), F32), vm((NC, R, 512), F32), vm((NC, R, 512), F32), vm((NC, R, 512), F32),
        vm((NC, 2, R, 512), BF16),
        *heads, *heads,
        vm((L, H), BF16), vm((L, H), BF16), vm((L, H), BF16), vm((L, H), BF16), vm((2, 4, 2, L, H), BF16),
        vm((L, 256), F32),
        vm((NC, 2, R, 384), F32), vm((NC, R, 384), F32), vm((NC, R, 384), BF16), vm((NC, R, 384), BF16),
        vm((NC, 2, R, 256), BF16), vm((L, 256), BF16), vm((NT, R, 256), BF16),
        vm((NC, 2, R, 256), BF16), vm((L, 256), BF16),
        vm((4, L, 256), F32),
        vm((4, 4, T, 256), BF16), vm((4, 4, T, 256), BF16), vm((4, 4, T, 256), BF16), vm((4, 4, T, 256), BF16),
        vm((256, H), F32), vm((256, H), F32), vm((256, W), BF16), vm((256, W), BF16),
        dma((16,)), dma((16,)), dma((16,)), dma((2, 2, 4)), dma((2, 2, 4)), dma((4,)), dma((4,)),
        dma((2, 4, 2)), dma((2, 4, 2)), dma((2, 4)), dma((2, 4)), dma((2, 4, 3)), dma((2, 4, 3)),
        dma((4, 3)), dma((4, 3)), dma((4,)), dma((4,)), dma((4, 2)), dma((4, 2)),
        dma((2, 4, 4)), dma((2, 4, 4)), dma((3,)), dma((3,)),
    ]
    hidden, down, up, small = pl.pallas_call(
        kernel,
        out_shape=(
            jax.ShapeDtypeStruct((T, W), F32),
            jax.ShapeDtypeStruct((192, W), F32),
            jax.ShapeDtypeStruct((64, W), F32),
            jax.ShapeDtypeStruct((256, H), F32),
        ),
        in_specs=[pl.BlockSpec(memory_space=pl.ANY)] * 13,
        out_specs=(pl.BlockSpec(memory_space=pltpu.VMEM),) * 4,
        scratch_shapes=scratch,
        compiler_params=pltpu.CompilerParams(
            collective_id=0, has_side_effects=True, vmem_limit_bytes=60 * 2**20
        ),
        name="adapter_backward",
    )(
        residual_input[0],
        block_output_gradient[0],
        norm_gain_vector.reshape(8, H),
        query_matrix[:, 0, :],
        output_matrix[0],
        keyvalue_matrix.reshape(2 * W, H),
        adapter_projection_down.T,
        adapter_output_up,
        adapter_query_up[:, 0, :],
        adapter_keyvalue_up.reshape(128, H),
        adapter_output_down[0].T,
        jnp.asarray(cosine),
        jnp.asarray(sine),
    )
    hidden, down, up, query_up, keyvalue_up, output_down = pl.pallas_call(
        hand_over,
        out_shape=(
            jax.ShapeDtypeStruct((T, W), F32),
            jax.ShapeDtypeStruct((192, W), F32),
            jax.ShapeDtypeStruct((64, W), F32),
            jax.ShapeDtypeStruct((64, H), F32),
            jax.ShapeDtypeStruct((128, H), F32),
            jax.ShapeDtypeStruct((64, H), F32),
        ),
        in_specs=[pl.BlockSpec(memory_space=pltpu.VMEM)] * 4,
        out_specs=(pl.BlockSpec(memory_space=pltpu.VMEM),) * 6,
        name="hand_over",
    )(hidden, down, up, small)
    return (
        hidden[None],
        down.T,
        query_up[:, None, :],
        keyvalue_up.reshape(64, 2, H),
        output_down.T[None],
        up,
    )


def solution(mesh):
    in_specs = (
        P("dp", "tensor", "fsdp"),
        P("dp", "tensor", "fsdp"),
        P("fsdp"),
        P("fsdp", "tensor", None),
        P("fsdp", None, "tensor"),
        P("tensor", None, "fsdp"),
        P("fsdp", None),
        P(None, "tensor", "fsdp"),
        P(None, None, "tensor"),
        P("tensor", "fsdp", None),
        P(None, "fsdp"),
    )
    out_specs = (
        P("dp", "tensor", "fsdp"),
        P("fsdp", None),
        P(None, "tensor", "fsdp"),
        P(None, None, "tensor"),
        P("tensor", "fsdp", None),
        P(None, "fsdp"),
    )
    return jax.shard_map(local, mesh=mesh, in_specs=in_specs, out_specs=out_specs, check_vma=False)
```

time: 168 us -> 125 us (0.74); the launches traced: 165 us -> 125 us
  Pallas kernels: 152 us -> 125 us
  other arithmetic: 7.71 us -> 0 us
  local copies, waits for them, and re-layouts: 4.14 us -> 0 us
    pallas_call x1, Pallas kernels: 152 us -> 122 us  [local(): pl.pallas_call(kernel, out_shape=(jax.ShapeDtypeStruct((T, W), F32), jax....]
    unnamed x4 -> x0, local copies, waits for them, and re-layouts: 2.6 us -> none
    mul x2 -> x0, other arithmetic: 2.59 us -> none  [the longest x1 1.67 us: local(): up * adapter_scale]
    pallas_call x0 -> x1, Pallas kernels: none -> 2.43 us  [local(): pl.pallas_call(hand_over, out_shape=(jax.ShapeDtypeStruct((T, W), F32), j...]
    transpose x1 -> x0, other arithmetic: 2.1 us -> none  [local(): return (hidden, (down * adapter_scale).T, small[:64, None, :], jnp.stack(...]
where the time goes in v2:
time: 125 us
  Pallas kernels  125 us (100%)
    pallas_call x1, Pallas kernels, local(): pl.pallas_call(kernel, out_shape=(jax.ShapeDtypeStruct((T, W), F32), jax....  122 us

profile of v2, /device:TPU:1, one launch (start us, length us, event | category | flops | bytes accessed | tf_op | source)
XLA Modules:
  0.0 125.4 jit_solution(17107748659595427672)
XLA Ops:
  0.6 122.3 %adapter_backward.1 = (f32[64,1024]{1,0:T(8,128)}, f32[192,1024]{1,0:T(8,128)}, f32[64,1024]{1,0:T(8,128)}, f32[256,128]{1,0:T(8,128)}) custom-call(bf16[64,1024]{1,0:T(8,128)(2,1)} %bitcast.25, bf16[64,1024]{1,0:T(8,128)(2,1)} %bitcast.26, f32[8,128]{1,0:T(8,128)} %bitcast.30, bf16[1024,2048]{1,0:T(8,128)(2,1)} %bitcast.21, bf16[2048,1024]{1,0:T(8,128)(2,1)} %bitcast.22, ...), custom_call_target="tpu_custom_call" | custom-call | tf_op jit(solution)/shard_map/adapter_backward/pallas_call | solution.py:766
  122.9 2.4 %hand_over.1 = (f32[64,1024]{1,0:T(8,128)}, f32[192,1024]{1,0:T(8,128)}, f32[64,1024]{1,0:T(8,128)}, f32[64,128]{1,0:T(8,128)}, f32[128,128]{1,0:T(8,128)}, /*index=5*/f32[64,128]{1,0:T(8,128)}) custom-call(f32[64,1024]{1,0:T(8,128)} %get-tuple-element.16.hid, f32[192,1024]{1,0:T(8,128)} %get-tuple-element.17.pd, f32[64,1024]{1,0:T(8,128)} %get-tuple-element.18.ou, ...), custom_call_target="tpu_custom_call" | custom-call | tf_op jit(solution)/shard_map/hand_over/pallas_call | solution.py:796

commit v3 on v2

--- a/solution.py
+++ b/solution.py
@@ -150,6 +150,14 @@
     squares = dot(ones, x_own * x_own, 1, 1, precision=lax.Precision.HIGHEST)
     ss_own[...] = jnp.concatenate([squares, squares], axis=1)
 
+    copies[5].wait()
+    copies[10].wait()
+    wkv_f[...] = wkv_in[...].astype(F32)
+    wkv[:, pl.ds(0, H)] = wkv_f[pl.ds(0, W, stride=2)].astype(BF16)
+    wkv[:, pl.ds(H, H)] = wkv_f[pl.ds(1, W, stride=2)].astype(BF16)
+    upkv_f[...] = upkv_in[...].astype(F32)
+    upk[pl.ds(128, 64)] = upkv_f[pl.ds(0, 64, stride=2)].astype(BF16)
+    upv[pl.ds(192, 64)] = upkv_f[pl.ds(1, 64, stride=2)].astype(BF16)
     pl.semaphore_wait(barrier, NF - 1 + NT - 1 + 1)
 
     def ring(buf, n):
@@ -273,7 +281,7 @@
     def q_product(rows, ci):
         return dot(nb[rows], wq[:, pl.ds(pl.multiple_of(ci * 256, 256), 256)], 1, 0)
 
-    a_chunks = [(0, 64), (64, 128), (192, 128), (320, 192)]
+    a_chunks = [(0, 64), (64, 128), (192, 128), (320, 128), (448, 64)]
     q_chunks = [(0, 192), (192, 128), (320, 128), (448, 64)]
     a1, a2, a3, a_total, a_finish = heads(
         a_product, a_chunks, 0, (a_acc_o, a_acc_s, a_ps_o, a_ps_s, a_pr_o, a_pr_s, a_xs, a_xr, a_ys, a_yr)
@@ -354,52 +362,49 @@
     g_arrive(1)
     g_start(2)
     a1(1, 0)
+    for i in (2, 4, 6, 7, 8, 9):
+        copies[i].wait()
     x_arrive(1)
     x_start(2)
     a1(1, 1)
-    a2(1)
-    a3(0)
-    for i in (2, 4, 5, 6, 7, 8, 9, 10):
-        copies[i].wait()
-    wkv_f[...] = wkv_in[...].astype(F32)
-    wkv[:, pl.ds(0, H)] = wkv_f[pl.ds(0, W, stride=2)].astype(BF16)
-    wkv[:, pl.ds(H, H)] = wkv_f[pl.ds(1, W, stride=2)].astype(BF16)
-    upkv_f[...] = upkv_in[...].astype(F32)
-    upk[pl.ds(128, 64)] = upkv_f[pl.ds(0, 64, stride=2)].astype(BF16)
-    upv[pl.ds(192, 64)] = upkv_f[pl.ds(1, 64, stride=2)].astype(BF16)
-    g_arrive(2)
-    g_start(3)
     wait_bytes(r_all.at[pl.ds(0, NT - 1)], grp_r.at[1])
     for slot in range(3):
         normalise(slot)
     kvl1(0)
+    q1(0, 0)
+    g_arrive(2)
+    g_start(3)
+    a2(1)
+    a3(0)
+    q1(0, 1)
+    kvl2(0)
+    a1(2, 0)
     x_arrive(2)
     x_start(3)
-    q1(0, 0)
-    q1(0, 1)
-    kvl2(0)
+    a1(2, 1)
     q2(0)
-    g_arrive(3)
-    g_start(4)
     normalise(3)
     normalise(4)
     kvl1(1)
-    a1(2, 0)
+    q1(1, 0)
+    g_arrive(3)
+    g_start(4)
+    q1(1, 1)
     a3(1)
-    a1(2, 1)
+    kvl2(1)
+    a2(2)
+    a1(3, 0)
     x_arrive(3)
     x_start(4)
-    kvl2(1)
-    q1(1, 0)
-    a2(2)
+    a1(3, 1)
+    q2(1)
     q3(0)
-    q1(1, 1)
-    q2(1)
     normalise(5)
     normalise(6)
     kvl1(2)
     q1(2, 0)
     g_arrive(4)
+    kvl2(2)
     bo_part[...] = dot(gb[...], gup[...], 1, 1).astype(BF16)
 
     @pl.loop(1, NF)
@@ -409,7 +414,7 @@
             bo_part.at[pl.ds(pl.multiple_of(fi * R, R), R)], bo_recv.at[i - 1], grp_s.at[2], grp_r.at[2], (d, fi, t)
         ).start()
 
-    kvl2(2)
+    a2(3)
     x_arrive(4)
     normalise(7)
     kvl1(3)
@@ -418,9 +423,13 @@
     q1(3, 0)
     q2(2)
     q1(3, 1)
+    a1(4, 0)
     q2(3)
+    a1(4, 1)
+    a3(2)
     q3(1)
-    a3(2)
+    a2(4)
+    a3(3)
     z_own = block(c)
     own_slots = pl.ds(pl.multiple_of(f * R, R), R)
     own_rows = pl.ds(pl.multiple_of(z_own * T + k * R, R), R)
@@ -444,12 +453,9 @@
     def _(i):
         rcopy(bo_ref, bo_ref, grp_s.at[3], grp_r.at[3], fdev(i)).start()
 
-    a1(3, 0)
     q3(2)
-    a2(3)
     q3(3)
-    a1(3, 1)
-    a3(3)
+    a3(4)
     wait_bytes(seven(kvl_all), grp_r.at[6])
     gather_mate(kvl_all, 7).start()
 
@@ -462,7 +468,7 @@
             dat[rows] = (part + adapter_scale * dot(bo_all[rows], odt[...], 1, 0)).astype(BF16)
 
     wait_bytes(bo_all.at[pl.ds(0, (NF - 1) * R)], grp_r.at[3])
-    for ch in range(3):
+    for ch in range(4):
         a_store(ch)
     gather_mate(kvl_all, 7).wait_recv()
     for ch, (r0, size) in enumerate(q_chunks):
@@ -473,7 +479,7 @@
             low = kvl_all[block(s), :, :, pl.ds(256, 256)].reshape(T, 256)
             query = part + adapter_scale * dot(low, upq[...], 1, 0)
             qrot[rows] = rotate(query, cosb[rows], sinb[rows]).astype(BF16)
-    a_store(3)
+    a_store(4)
 
     scale = 1.0 / math.sqrt(H)
     for i in range(4):
@@ -542,13 +548,13 @@
     p1_copy = rcopy(p1_part.at[:, 1 - k], p1_pair, grp_s.at[8], grp_r.at[8], mate)
     p1_copy.start()
     sm_own[pl.ds(192, 64)] = dot(bo_all[...], attn[...], 0, 0)[:64]
+    all_low = kvl_all[:, :, :, pl.ds(256, 256)].reshape(L, 256)
+    sm_own[pl.ds(0, 64)] = dot(all_low, dq_own[...], 0, 0)[:64]
     p1_copy.wait_recv()
     for s in range(NC):
         p1_send[s] = (p1_part[s, k] + p1_pair[s]).astype(BF16)
         to_chip(p1_send, p1_recv, s, 9)
     dq_send(1)
-    all_low = kvl_all[:, :, :, pl.ds(256, 256)].reshape(L, 256)
-    sm_own[pl.ds(0, 64)] = dot(all_low, dq_own[...], 0, 0)[:64]
     dq_forward_x(0)
     wait_bytes(p1_recv.at[pl.ds(0, NC - 1)], grp_r.at[9])
     total = chip_total(p1_part[c, k] + p1_pair[c], p1_recv)
@@ -567,18 +573,20 @@
     def _(i):
         rcopy(p2_all.at[t], p2_all.at[t], grp_s.at[12], grp_r.at[12], zdev(i)).start()
 
-    dq_forward_core(0)
-    dq_forward_x(1)
     dq_send(2)
     dq_send(3)
+    dq_forward_x(1)
     wait_bytes(seven(dkv_all), grp_r.at[10])
     gather_mate(dkv_all, 11).start()
+    dq_forward_core(0)
     wait_bytes(p2_all.at[pl.ds(0, NT - 1)], grp_r.at[12])
     total = p2_all[0].astype(F32)
     for i in range(1, NT):
         total = total + p2_all[i].astype(F32)
     back_all[c, k] = total.astype(BF16)
     gather_chips(back_all, c, 13)
+    dq_forward_x(2)
+    dq_forward_core(1)
     gather_mate(dkv_all, 11).wait_recv()
     for s in range(NT):
         dkv_slot[slot_rows(s)] = dkv_all[block(s)].reshape(T, 256)
@@ -602,16 +610,8 @@
         send[j, s] = value.astype(BF16)
         rs_copy(j, way, s).start()
 
-    for ch in range(4):
+    def z_products(ch):
         rows = pl.ds(*z_chunks[ch])
-        if ch == 1:
-            dq_forward_core(1)
-            dq_forward_x(2)
-        if ch == 2:
-            dq_forward_core(2)
-            dq_forward_x(3)
-        if ch == 3:
-            dq_forward_core(3)
         dqc_copy(ch, 0).wait_recv()
         dqc_copy(ch, 1).wait_recv()
         dq = jnp.concatenate([dq_all[i // 8, i // 2 % 4, i % 2, rows] for i in range(NF)], axis=1)
@@ -622,10 +622,12 @@
                 s = ch if j % 2 == way else ch - 1
                 if s >= 0:
                     rs_step(j, way, s)
-        if ch == 1:
-            wait_bytes(seven(back_all), grp_r.at[13])
-            gather_mate(back_all, 14).start()
-
+
+    z_products(0)
+    dq_forward_x(3)
+    wait_bytes(seven(back_all), grp_r.at[13])
+    gather_mate(back_all, 14).start()
+    z_products(1)
     gather_mate(back_all, 14).wait_recv()
     for s in range(NT):
         back_slot[slot_rows(s)] = back_all[block(s)].reshape(T, 256)
@@ -637,11 +639,15 @@
             ex_own[pl.ds(64, 64)] = dot(back_slot[:, rows], gb[...], 0, 0)[64:].astype(BF16)
         halves.append(rcopy(ex_own.at[rows], ex_recv.at[rows], dp_s.at[1 + i], dp_r.at[1 + i], other))
         halves[i].start()
+    dq_forward_core(2)
+    z_products(2)
+    dq_forward_core(3)
     kv_up = dot(all_low, dkv_all[...].reshape(L, 256), 0, 0)
     sm_own[pl.ds(64, 64)] = kv_up[128:192, :H]
     sm_own[pl.ds(128, 64)] = kv_up[192:, H:]
     small = rcopy(sm_own, sm_recv, dp_s.at[0], dp_r.at[0], other)
     small.start()
+    z_products(3)
 
     inverse = column(r_all[t])
     xhat = x_own * inverse
@@ -759,7 +765,7 @@
         vm((4, 4, T, 256), BF16), vm((4, 4, T, 256), BF16), vm((4, 4, T, 256), BF16), vm((4, 4, T, 256), BF16),
         vm((256, H), F32), vm((256, H), F32), vm((256, W), BF16), vm((256, W), BF16),
         dma((16,)), dma((16,)), dma((16,)), dma((2, 2, 4)), dma((2, 2, 4)), dma((4,)), dma((4,)),
-        dma((2, 4, 2)), dma((2, 4, 2)), dma((2, 4)), dma((2, 4)), dma((2, 4, 3)), dma((2, 4, 3)),
+        dma((2, 5, 2)), dma((2, 5, 2)), dma((2, 5)), dma((2, 5)), dma((2, 5, 3)), dma((2, 5, 3)),
         dma((4, 3)), dma((4, 3)), dma((4,)), dma((4,)), dma((4, 2)), dma((4, 2)),
         dma((2, 4, 4)), dma((2, 4, 4)), dma((3,)), dma((3,)),
     ]

time: 125 us -> 111 us (0.89)
  Pallas kernels: 125 us -> 110 us
    pallas_call x1, Pallas kernels: 122 us -> 107 us  [local(): pl.pallas_call(kernel, out_shape=(jax.ShapeDtypeStruct((T, W), F32), jax....]
where the time goes in v3:
time: 111 us; the launch traced here: 110 us
  Pallas kernels  110 us (99%)
    pallas_call x1, Pallas kernels, local(): pl.pallas_call(kernel, out_shape=(jax.ShapeDtypeStruct((T, W), F32), jax....  107 us
    pallas_call x1, Pallas kernels, local(): pl.pallas_call(hand_over, out_shape=(jax.ShapeDtypeStruct((T, W), F32), j...  2.43 us

profile of v3, /device:TPU:1, one launch (start us, length us, event | category | flops | bytes accessed | tf_op | source)
XLA Modules:
  0.0 110.5 jit_solution(14948703481461291964)
XLA Ops:
  0.6 107.4 %adapter_backward.1 = (f32[64,1024]{1,0:T(8,128)}, f32[192,1024]{1,0:T(8,128)}, f32[64,1024]{1,0:T(8,128)}, f32[256,128]{1,0:T(8,128)}) custom-call(bf16[64,1024]{1,0:T(8,128)(2,1)} %bitcast.25, bf16[64,1024]{1,0:T(8,128)(2,1)} %bitcast.26, f32[8,128]{1,0:T(8,128)} %bitcast.30, bf16[1024,2048]{1,0:T(8,128)(2,1)} %bitcast.21, bf16[2048,1024]{1,0:T(8,128)(2,1)} %bitcast.22, ...), custom_call_target="tpu_custom_call" | custom-call | tf_op jit(solution)/shard_map/adapter_backward/pallas_call | solution.py:772
  108.0 2.4 %hand_over.1 = (f32[64,1024]{1,0:T(8,128)}, f32[192,1024]{1,0:T(8,128)}, f32[64,1024]{1,0:T(8,128)}, f32[64,128]{1,0:T(8,128)}, f32[128,128]{1,0:T(8,128)}, /*index=5*/f32[64,128]{1,0:T(8,128)}) custom-call(f32[64,1024]{1,0:T(8,128)} %get-tuple-element.16.hid, f32[192,1024]{1,0:T(8,128)} %get-tuple-element.17.pd, f32[64,1024]{1,0:T(8,128)} %get-tuple-element.18.ou, ...), custom_call_target="tpu_custom_call" | custom-call | tf_op jit(solution)/shard_map/hand_over/pallas_call | solution.py:802

commit v4 on v3

--- a/solution.py
+++ b/solution.py
@@ -303,17 +303,17 @@
         kvl_part[pl.ds(s0, n), :, :, pl.ds(256, 256)] = dot(nb[rows], dwt[...], 1, 1).reshape(n, 2, R, 256)
         kvl_copy(ch).start()
 
-    def to_chip(send, recv, s, n):
-        @pl.when(s != c)
+    def to_chip(send, recv, s, n, chip):
+        @pl.when(chip != c)
         def _():
-            rcopy(send.at[s], recv.at[c], grp_s.at[n], grp_r.at[n], (d, 2 * s + k, t)).start()
+            rcopy(send.at[s], recv.at[c], grp_s.at[n], grp_r.at[n], (d, 2 * chip + k, t)).start()
 
     def kvl2(ch):
         s0, n = q_chunks[ch][0] // T, q_chunks[ch][1] // T
         kvl_copy(ch).wait_recv()
         for s in range(s0, s0 + n):
             kvl_send[s] = kvl_part[s, k] + kvl_pair[s]
-            to_chip(kvl_send, kvl_recv, s, 5)
+            to_chip(kvl_send, kvl_recv, s, 5, lax.rem(s + 4 * k, NC))
 
     def chip_total(own, recv):
         def add(i, total):
@@ -430,13 +430,15 @@
     q3(1)
     a2(4)
     a3(3)
-    z_own = block(c)
     own_slots = pl.ds(pl.multiple_of(f * R, R), R)
+    bo_rows = pl.ds(pl.multiple_of(block(c) * T + k * R, R), R)
+    kv_slot = lax.rem(c + 4 * k, NC)
+    z_own = block(kv_slot)
     own_rows = pl.ds(pl.multiple_of(z_own * T + k * R, R), R)
     for i in range(11, 15):
         copies[i].wait()
     wait_bytes(kvl_recv.at[pl.ds(0, NC - 1)], grp_r.at[5])
-    total = chip_total(kvl_send[c], kvl_recv)
+    total = chip_total(kvl_send[kv_slot], kvl_recv)
     low = total[:, 256:].astype(BF16)
     keys = total[:, :H] + adapter_scale * dot(low, upk[...], 1, 0)
     values = total[:, H:256] + adapter_scale * dot(low, upv[...], 1, 0)
@@ -446,8 +448,8 @@
     kvl_all[z_own, k, :, pl.ds(256, 256)] = low
     gather_chips(kvl_all, z_own, 6)
     wait_bytes(bo_recv, grp_r.at[2])
-    bo_all[own_rows] = total_f(bo_part[own_slots], bo_recv).astype(BF16)
-    bo_ref = bo_all.at[own_rows]
+    bo_all[bo_rows] = total_f(bo_part[own_slots], bo_recv).astype(BF16)
+    bo_ref = bo_all.at[bo_rows]
 
     @pl.loop(1, NF)
     def _(i):
@@ -553,7 +555,7 @@
     p1_copy.wait_recv()
     for s in range(NC):
         p1_send[s] = (p1_part[s, k] + p1_pair[s]).astype(BF16)
-        to_chip(p1_send, p1_recv, s, 9)
+        to_chip(p1_send, p1_recv, s, 9, s)
     dq_send(1)
     dq_forward_x(0)
     wait_bytes(p1_recv.at[pl.ds(0, NC - 1)], grp_r.at[9])
@@ -627,7 +629,6 @@
     dq_forward_x(3)
     wait_bytes(seven(back_all), grp_r.at[13])
     gather_mate(back_all, 14).start()
-    z_products(1)
     gather_mate(back_all, 14).wait_recv()
     for s in range(NT):
         back_slot[slot_rows(s)] = back_all[block(s)].reshape(T, 256)
@@ -639,6 +640,7 @@
             ex_own[pl.ds(64, 64)] = dot(back_slot[:, rows], gb[...], 0, 0)[64:].astype(BF16)
         halves.append(rcopy(ex_own.at[rows], ex_recv.at[rows], dp_s.at[1 + i], dp_r.at[1 + i], other))
         halves[i].start()
+    z_products(1)
     dq_forward_core(2)
     z_products(2)
     dq_forward_core(3)

time: 111 us -> 109 us (0.982)
  Pallas kernels: 110 us -> 108 us
    pallas_call x1, Pallas kernels: 107 us -> 105 us  [local(): pl.pallas_call(kernel, out_shape=(jax.ShapeDtypeStruct((T, W), F32), jax....]
where the time goes in v4:
time: 109 us; the launch traced here: 108 us
  Pallas kernels  108 us (99%)
    pallas_call x1, Pallas kernels, local(): pl.pallas_call(kernel, out_shape=(jax.ShapeDtypeStruct((T, W), F32), jax....  105 us
    pallas_call x1, Pallas kernels, local(): pl.pallas_call(hand_over, out_shape=(jax.ShapeDtypeStruct((T, W), F32), j...  2.43 us

profile of v4, /device:TPU:1, one launch (start us, length us, event | category | flops | bytes accessed | tf_op | source)
XLA Modules:
  0.0 108.4 jit_solution(9352798212276354591)
XLA Ops:
  0.6 105.3 %adapter_backward.1 = (f32[64,1024]{1,0:T(8,128)}, f32[192,1024]{1,0:T(8,128)}, f32[64,1024]{1,0:T(8,128)}, f32[256,128]{1,0:T(8,128)}) custom-call(bf16[64,1024]{1,0:T(8,128)(2,1)} %bitcast.25, bf16[64,1024]{1,0:T(8,128)(2,1)} %bitcast.26, f32[8,128]{1,0:T(8,128)} %bitcast.30, bf16[1024,2048]{1,0:T(8,128)(2,1)} %bitcast.21, bf16[2048,1024]{1,0:T(8,128)(2,1)} %bitcast.22, ...), custom_call_target="tpu_custom_call" | custom-call | tf_op jit(solution)/shard_map/adapter_backward/pallas_call | solution.py:774
  106.0 2.4 %hand_over.1 = (f32[64,1024]{1,0:T(8,128)}, f32[192,1024]{1,0:T(8,128)}, f32[64,1024]{1,0:T(8,128)}, f32[64,128]{1,0:T(8,128)}, f32[128,128]{1,0:T(8,128)}, /*index=5*/f32[64,128]{1,0:T(8,128)}) custom-call(f32[64,1024]{1,0:T(8,128)} %get-tuple-element.16.hid, f32[192,1024]{1,0:T(8,128)} %get-tuple-element.17.pd, f32[64,1024]{1,0:T(8,128)} %get-tuple-element.18.ou, ...), custom_call_target="tpu_custom_call" | custom-call | tf_op jit(solution)/shard_map/hand_over/pallas_call | solution.py:804
